TPU v7x, 32 devices: a whole 2x2x4 slice. The times are simulated.
32 devices in a mesh: dom: 8 (over z, core), rows: 4 (over y, x).
Axes of the slice: x: 2, y: 2, z: 4, core: 2. Of those that a mesh axis runs over, the one named last changes fastest.
Arguments:
- features: bfloat16 [16384, 256], P(('dom', 'rows')), may hold values from -6 to 6
- weight: bfloat16 [256, 256], replicated, may hold values from -0.375 to 0.375
- tile_values: bfloat16 [32, 5, 4, 128, 128], P(('dom', 'rows')), may hold values from -0.1875 to 0.1875
- tile_source: int32 [32, 5, 4], P(('dom', 'rows')), may hold values from 0 to 3
- tile_slot: int32 [32, 5, 4], P(('dom', 'rows')), may hold values from 0 to 7
- slot_block: int32 [32, 8], P(('dom', 'rows')), may hold values from 0 to 3
- tile_count: int32 [32, 5], P(('dom', 'rows')), may hold values from 1 to 4
- cotangent: bfloat16 [16384, 256], P(('dom', 'rows')), may hold values from -6 to 6
Outputs:
- activations: bfloat16 [16384, 256], P(('dom', 'rows'))
- feature_grad: bfloat16 [16384, 256], P(('dom', 'rows'))
- weight_grad: float32 [256, 256], replicated
Inputs may be any that keep to these rules, and one draw needn't show every extreme that they name: Tiles of index tile_count[g, k] and above at offset index k are padding; their tile_values, tile_source and tile_slot count for nothing.
All inputs are finite; a program needn't handle non-finite values.
Results may differ from a plain program's by a relative error of at most 0.019.
Values may be sent and summed in bfloat16 or wider, within the bound.
A program may use at most 64 MiB of HBM per device.

v0:
```python
import jax
import jax.numpy as jnp
from jax import lax
from jax.sharding import PartitionSpec as P

BLOCK = 128
HALF = 2
CAP = 2


def shifted(value, axis, steps):
    count = lax.axis_size(axis)
    pairs = [(source, (source + steps) % count) for source in range(count)]
    return lax.ppermute(value, axis, pairs)


def pass_features(visiting, offset_by):
    return shifted(visiting, "dom", offset_by)


def pass_sums(carried, offset_by):
    return shifted(carried, "dom", offset_by)


def per_device(
    features, weight, tile_values, tile_source, tile_slot, slot_block, tile_count, cotangent
):
    channels = features.shape[1]
    blocks_dev = features.shape[0] // BLOCK
    row_count = lax.axis_size("rows")
    values = tile_values[0]
    sources = tile_source[0]
    slot_ids = tile_slot[0]
    targets = slot_block[0]
    counts = tile_count[0]
    num_steps = values.shape[0]
    tiles_step = values.shape[1]
    slot_total = targets.shape[0]
    reach = HALF
    live_mask = jnp.arange(tiles_step, dtype=jnp.int32)[None, :] < counts[:, None]
    slot_onehot = (
        (slot_ids[..., None] == jnp.arange(slot_total, dtype=jnp.int32)) & live_mask[..., None]
    ).astype(jnp.float32)
    source_onehot = (
        (sources[..., None] == jnp.arange(blocks_dev, dtype=jnp.int32)) & live_mask[..., None]
    ).astype(jnp.float32)
    own_blocks = features.reshape(blocks_dev, BLOCK, channels)
    products = [None] * num_steps
    visiting = pass_features(own_blocks, reach)
    for step_idx in range(num_steps):
        if step_idx > 0:
            visiting = pass_features(visiting, -1)
        tile_picked = jnp.take(visiting, sources[step_idx], axis=0)
        products[step_idx] = jnp.einsum(
            "tij,tjf->tif", values[step_idx], tile_picked, preferred_element_type=jnp.float32
        )
    stacked = jnp.concatenate(products, axis=0)
    slot_sums = jnp.einsum("ts,tif->sif", slot_onehot.reshape(-1, slot_total), stacked)
    partials = slot_sums.astype(jnp.bfloat16).reshape(row_count, CAP, BLOCK, channels)
    ids_wire = targets.reshape(row_count, CAP).astype(jnp.bfloat16)
    received, received_ids = (
        lax.all_to_all(partials, "rows", split_axis=0, concat_axis=0, tiled=True),
        lax.all_to_all(ids_wire, "rows", split_axis=0, concat_axis=0, tiled=True),
    )
    block_codes = jnp.arange(blocks_dev, dtype=jnp.int32).astype(jnp.bfloat16)
    owner_onehot = (received_ids[..., None] == block_codes).astype(jnp.bfloat16)
    aggregate = jnp.einsum(
        "rcb,rcif->bif", owner_onehot, received, preferred_element_type=jnp.float32
    )
    aggregate = aggregate.astype(jnp.bfloat16).reshape(blocks_dev * BLOCK, channels)
    pre_act = jnp.dot(aggregate, weight, preferred_element_type=jnp.float32)
    activations = jax.nn.silu(pre_act).astype(jnp.bfloat16)
    sigmoid_pre = jax.nn.sigmoid(pre_act)
    slope_factor = sigmoid_pre * (1.0 + pre_act * (1.0 - sigmoid_pre))
    pre_grad = (cotangent.astype(jnp.float32) * slope_factor).astype(jnp.bfloat16)
    local_grad = lax.dot_general(
        aggregate, pre_grad, (((0,), (0,)), ((), ())), preferred_element_type=jnp.float32
    )
    weight_grad = lax.psum(local_grad, ("dom", "rows"))
    agg_grad = lax.dot_general(
        pre_grad, weight, (((1,), (1,)), ((), ())), preferred_element_type=jnp.float32
    )
    agg_grad = agg_grad.astype(jnp.bfloat16).reshape(blocks_dev, BLOCK, channels)
    reply_blocks = jnp.take(agg_grad, received_ids.astype(jnp.int32), axis=0)
    returned = lax.all_to_all(
        reply_blocks, "rows", split_axis=0, concat_axis=0, tiled=True
    ).reshape(slot_total, BLOCK, channels)

    def source_terms(step_idx):
        picked = jnp.take(returned, slot_ids[step_idx], axis=0)
        product = jnp.einsum(
            "tji,tjf->tif", values[step_idx], picked, preferred_element_type=jnp.float32
        )
        return jnp.einsum("tb,tif->bif", source_onehot[step_idx], product)

    carried = source_terms(num_steps - 1)
    for step_idx in range(num_steps - 2, -1, -1):
        carried = pass_sums(carried, 1) + source_terms(step_idx)
    source_grad = pass_sums(carried, -reach)
    feature_grad = source_grad.astype(jnp.bfloat16).reshape(blocks_dev * BLOCK, channels)
    return (activations, feature_grad, weight_grad)


def solution(mesh):
    return jax.shard_map(
        per_device,
        mesh=mesh,
        in_specs=(
            P(("dom", "rows"), None),
            P(),
            P(("dom", "rows"), None, None, None, None),
            P(("dom", "rows"), None, None),
            P(("dom", "rows"), None, None),
            P(("dom", "rows"), None),
            P(("dom", "rows"), None),
            P(("dom", "rows"), None),
        ),
        out_specs=(P(("dom", "rows"), None), P(("dom", "rows"), None), P()),
        check_vma=False,
    )
```

profile of v0, /device:TPU:0, one launch (start us, length us, event | category | flops | bytes accessed | tf_op | source)
XLA Modules:
  0.0 258.5 jit_solution(6110365038236325415)
XLA Ops:
  7.2 3.1 %collective-permute-start = (bf16[4,128,256]{2,1,0:T(8,128)(2,1)}, bf16[4,128,256]{2,1,0:T(8,128)(2,1)S(1)}, u32[]{:S(2)}, u32[]{:S(2)}) collective-permute-start(bf16[4,128,256]{2,1,0:T(8,128)(2,1)} %bitcast.132), channel_id=1, source_target_pairs={{0,8},{4,12},{8,16},{12,20},{16,24},{20,28},{24,0},{28,4},{1,9},{5... | collective-permute-start | bytes 786440 | tf_op jit(solution)/shard_map/ppermute | solution.py:14
  10.3 0.7 convert_reduce_fusion
  10.9 0.7 convert_element_type.75
  11.6 3.7 %all-to-all-start = ((bf16[4,1,2]{2,1,0:T(2,128)(2,1)}), bf16[4,1,2]{2,1,0:T(2,128)(2,1)S(1)}, u32[]{:S(2)}, u32[]{:S(2)}) async-start(bf16[4,1,2]{2,1,0:T(2,128)(2,1)} %convert_element_type.75), calls=%async_computation | async-start | bytes 4096 | tf_op jit(solution)/shard_map/all_to_all | solution.py:63
  15.3 1.1 slice_reduce_fusion.5
  16.6 1.1 slice_reduce_fusion
  17.8 1.0 collective-permute-done
  18.8 0.3 collective-permute-start.1
  19.2 0.7 iota_compare_fusion.1
  19.9 3.2 %collective-permute-done.1 = bf16[4,128,256]{2,1,0:T(8,128)(2,1)S(1)} collective-permute-done((bf16[4,128,256]{2,1,0:T(8,128)(2,1)S(1)}, bf16[4,128,256]{2,1,0:T(8,128)(2,1)S(1)}, u32[]{:S(2)}, u32[]{:S(2)}) %collective-permute-start.1) | collective-permute-done | bytes 262176 | tf_op jit(solution)/shard_map/ppermute | solution.py:14
  23.0 3.7 %collective-permute-start.2 = (bf16[4,128,256]{2,1,0:T(8,128)(2,1)S(1)}, bf16[4,128,256]{2,1,0:T(8,128)(2,1)S(1)}, u32[]{:S(2)}, u32[]{:S(2)}) collective-permute-start(bf16[4,128,256]{2,1,0:T(8,128)(2,1)S(1)} %collective-permute-done.1), channel_id=1, source_target_pairs={{0,28},{4,0},{8,4},{12,8},{16,12},{20,16},{24,20},{28,24},{1,29},{... | collective-permute-start | bytes 786440 | tf_op jit(solution)/shard_map/ppermute | solution.py:14
  26.7 0.8 copy.93
  27.7 0.8 copy.103
  28.6 0.6 gather_fusion.1
  29.1 1.5 collective-permute-done.2
  30.6 3.7 %collective-permute-start.3 = (bf16[4,128,256]{2,1,0:T(8,128)(2,1)S(1)}, bf16[4,128,256]{2,1,0:T(8,128)(2,1)S(1)}, u32[]{:S(2)}, u32[]{:S(2)}) collective-permute-start(bf16[4,128,256]{2,1,0:T(8,128)(2,1)S(1)} %collective-permute-done.2), channel_id=1, source_target_pairs={{0,28},{4,0},{8,4},{12,8},{16,12},{20,16},{24,20},{28,24},{1,29},{... | collective-permute-start | bytes 786440 | tf_op jit(solution)/shard_map/ppermute | solution.py:14
  34.3 1.9 fusion.4
  36.3 0.6 gather_fusion.2
  36.9 1.1 fusion.3
  37.9 0.6 gather_fusion.3
  38.5 3.4 %collective-permute-start.4 = (bf16[4,128,256]{2,1,0:T(8,128)(2,1)S(1)}, bf16[4,128,256]{2,1,0:T(8,128)(2,1)S(1)}, u32[]{:S(2)}, u32[]{:S(2)}) collective-permute-start(bf16[4,128,256]{2,1,0:T(8,128)(2,1)S(1)} %collective-permute-done.3), channel_id=1, source_target_pairs={{0,28},{4,0},{8,4},{12,8},{16,12},{20,16},{24,20},{28,24},{1,29},{... | collective-permute-start | bytes 786440 | tf_op jit(solution)/shard_map/ppermute | solution.py:14
  41.9 1.1 fusion.2
  43.0 0.6 gather_fusion.4
  43.6 1.1 fusion.1
  44.6 1.2 collective-permute-done.4
  45.8 0.6 gather_fusion.5
  46.4 1.1 fusion
  47.5 2.1 copy.99
  49.6 0.4 convolution_convert_fusion
  50.2 1.1 copy.100
  51.3 4.0 %all-to-all-start.1 = ((bf16[4,2,128,256]{3,1,2,0:T(2,128)(2,1)}), bf16[4,2,128,256]{3,1,2,0:T(2,128)(2,1)S(1)}, u32[]{:S(2)}, u32[]{:S(2)}) async-start(bf16[4,2,128,256]{3,1,2,0:T(2,128)(2,1)} %copy.100), calls=%async_computation.1 | async-start | bytes 1048576 | tf_op jit(solution)/shard_map/all_to_all | solution.py:62
  55.7 6.3 %all-to-all-done.1 = bf16[4,2,128,256]{3,1,2,0:T(2,128)(2,1)S(1)} async-done(((bf16[4,2,128,256]{3,1,2,0:T(2,128)(2,1)}), bf16[4,2,128,256]{3,1,2,0:T(2,128)(2,1)S(1)}, u32[]{:S(2)}, u32[]{:S(2)}) %all-to-all-start.1) | async-done | bytes 524320 | tf_op jit(solution)/shard_map/all_to_all | solution.py:62
  62.0 0.8 fusion.5
  62.8 1.1 multiply_convert_fusion
  64.2 0.6 gather_fusion
  64.8 0.9 broadcast_select_fusion
  65.7 3.5 %all-to-all-start.2 = ((bf16[4,2,128,256]{3,2,1,0:T(8,128)(2,1)}), bf16[4,2,128,256]{3,2,1,0:T(8,128)(2,1)S(1)}, u32[]{:S(2)}, u32[]{:S(2)}) async-start(bf16[4,2,128,256]{3,2,1,0:T(8,128)(2,1)} %broadcast_select_fusion), calls=%async_computation.2 | async-start | bytes 1048576 | tf_op jit(solution)/shard_map/all_to_all | solution.py:85
  69.3 6.4 %all-to-all-done.2 = bf16[4,2,128,256]{3,2,1,0:T(8,128)(2,1)S(1)} async-done(((bf16[4,2,128,256]{3,2,1,0:T(8,128)(2,1)}), bf16[4,2,128,256]{3,2,1,0:T(8,128)(2,1)S(1)}, u32[]{:S(2)}, u32[]{:S(2)}) %all-to-all-start.2) | async-done | bytes 524320 | tf_op jit(solution)/shard_map/all_to_all | solution.py:85
  75.7 0.6 gather_fusion.6
  76.3 0.3 convolution_bitcast_fusion.5
  76.8 0.3 fusion.67
  77.3 0.6 gather_fusion.7
  77.9 0.3 convolution_bitcast_fusion.4
  78.4 9.2 %collective-permute-done.5 = f32[4,128,256]{2,0,1:T(4,128)S(1)} collective-permute-done((f32[4,128,256]{2,0,1:T(4,128)S(1)}, f32[4,128,256]{2,0,1:T(4,128)S(1)}, u32[]{:S(2)}, u32[]{:S(2)}) %collective-permute-start.5) | collective-permute-done | bytes 524320 | tf_op jit(solution)/shard_map/ppermute | solution.py:14
  87.6 0.3 convolution_add_fusion
  88.1 0.6 gather_fusion.8
  88.7 0.3 convolution_bitcast_fusion.3
  89.2 0.3 fusion.66
  89.6 9.0 %collective-permute-done.6 = f32[4,128,256]{2,0,1:T(4,128)} collective-permute-done((f32[4,128,256]{2,0,1:T(4,128)S(1)}, f32[4,128,256]{2,0,1:T(4,128)}, u32[]{:S(2)}, u32[]{:S(2)}) %collective-permute-start.6) | collective-permute-done | bytes 524320 | tf_op jit(solution)/shard_map/ppermute | solution.py:14
  98.6 1.2 add.48
  99.8 0.6 gather_fusion.9
  100.4 0.3 convolution_bitcast_fusion.2
  100.9 0.3 fusion.65
  101.3 9.0 %collective-permute-done.7 = f32[4,128,256]{2,0,1:T(4,128)} collective-permute-done((f32[4,128,256]{2,0,1:T(4,128)S(1)}, f32[4,128,256]{2,0,1:T(4,128)}, u32[]{:S(2)}, u32[]{:S(2)}) %collective-permute-start.7) | collective-permute-done | bytes 524320 | tf_op jit(solution)/shard_map/ppermute | solution.py:14
  110.3 1.2 add.49
  111.6 0.6 gather_fusion.10
  112.1 0.3 convolution_bitcast_fusion.1
  112.7 0.3 fusion.64
  113.0 11.8 %collective-permute-done.8 = f32[4,128,256]{2,0,1:T(4,128)S(1)} collective-permute-done((f32[4,128,256]{2,0,1:T(4,128)S(1)}, f32[4,128,256]{2,0,1:T(4,128)S(1)}, u32[]{:S(2)}, u32[]{:S(2)}) %collective-permute-start.8) | collective-permute-done | bytes 524320 | tf_op jit(solution)/shard_map/ppermute | solution.py:14
  125.1 1.0 fusion.81
  126.1 5.4 %collective-permute-done.9 = bf16[4,128,256]{2,0,1:T(4,128)(2,1)S(1)} collective-permute-done((bf16[4,128,256]{2,0,1:T(4,128)(2,1)S(1)}, bf16[4,128,256]{2,0,1:T(4,128)(2,1)S(1)}, u32[]{:S(2)}, u32[]{:S(2)}) %collective-permute-start.9) | collective-permute-done | bytes 262176 | tf_op jit(solution)/shard_map/ppermute | solution.py:14
  131.4 0.7 copy.122
  132.1 117.8 %all-reduce.2.cloned.1.call-done = f32[256,256]{1,0:T(8,128)} async-done(((f32[256,256]{1,0:T(8,128)}), f32[256,256]{1,0:T(8,128)}) %all-reduce.2.cloned.1.call-update) | async-done | bytes 262160 | tf_op jit(solution)/shard_map/psum | solution.py:79
  250.0 1.7 copy.151
  (61 shorter events, 2.8 us)
Async XLA Ops:
  7.2 55.6 %copy-start = (bf16[256,256]{1,0:T(8,128)(2,1)S(1)}, bf16[256,256]{1,0:T(8,128)(2,1)}, u32[]{:S(2)}) copy-start(bf16[256,256]{1,0:T(8,128)(2,1)} %param.13) | copy-start | bytes 393220
  7.2 29.7 %copy-start.1 = (bf16[1,5,4,128,128]{4,3,2,1,0:T(8,128)(2,1)S(1)}, bf16[1,5,4,128,128]{4,3,2,1,0:T(8,128)(2,1)}, u32[]{:S(2)}) copy-start(bf16[1,5,4,128,128]{4,3,2,1,0:T(8,128)(2,1)} %param.14) | copy-start | bytes 1966084
  7.2 11.6 %collective-permute-start = (bf16[4,128,256]{2,1,0:T(8,128)(2,1)}, bf16[4,128,256]{2,1,0:T(8,128)(2,1)S(1)}, u32[]{:S(2)}, u32[]{:S(2)}) collective-permute-start(bf16[4,128,256]{2,1,0:T(8,128)(2,1)} %bitcast.132), channel_id=1, source_target_pairs={{0,8},{4,12},{8,16},{12,20},{16,24},{20,28},{24,0},{28,4},{1,9},{5... | collective-permute-start | bytes 786440 | tf_op jit(solution)/shard_map/ppermute | solution.py:14
  11.6 16.9 %all-to-all-start = ((bf16[4,1,2]{2,1,0:T(2,128)(2,1)}), bf16[4,1,2]{2,1,0:T(2,128)(2,1)S(1)}, u32[]{:S(2)}, u32[]{:S(2)}) async-start(bf16[4,1,2]{2,1,0:T(2,128)(2,1)} %convert_element_type.75), calls=%async_computation | async-start | bytes 4096 | tf_op jit(solution)/shard_map/all_to_all | solution.py:63
  18.8 4.2 %collective-permute-start.1 = (bf16[4,128,256]{2,1,0:T(8,128)(2,1)S(1)}, bf16[4,128,256]{2,1,0:T(8,128)(2,1)S(1)}, u32[]{:S(2)}, u32[]{:S(2)}) collective-permute-start(bf16[4,128,256]{2,1,0:T(8,128)(2,1)S(1)} %collective-permute-done), channel_id=1, source_target_pairs={{0,28},{4,0},{8,4},{12,8},{16,12},{20,16},{24,20},{28,24},{1,29},{... | collective-permute-start | bytes 786440 | tf_op jit(solution)/shard_map/ppermute | solution.py:14
  23.0 7.6 %collective-permute-start.2 = (bf16[4,128,256]{2,1,0:T(8,128)(2,1)S(1)}, bf16[4,128,256]{2,1,0:T(8,128)(2,1)S(1)}, u32[]{:S(2)}, u32[]{:S(2)}) collective-permute-start(bf16[4,128,256]{2,1,0:T(8,128)(2,1)S(1)} %collective-permute-done.1), channel_id=1, source_target_pairs={{0,28},{4,0},{8,4},{12,8},{16,12},{20,16},{24,20},{28,24},{1,29},{... | collective-permute-start | bytes 786440 | tf_op jit(solution)/shard_map/ppermute | solution.py:14
  30.6 7.9 %collective-permute-start.3 = (bf16[4,128,256]{2,1,0:T(8,128)(2,1)S(1)}, bf16[4,128,256]{2,1,0:T(8,128)(2,1)S(1)}, u32[]{:S(2)}, u32[]{:S(2)}) collective-permute-start(bf16[4,128,256]{2,1,0:T(8,128)(2,1)S(1)} %collective-permute-done.2), channel_id=1, source_target_pairs={{0,28},{4,0},{8,4},{12,8},{16,12},{20,16},{24,20},{28,24},{1,29},{... | collective-permute-start | bytes 786440 | tf_op jit(solution)/shard_map/ppermute | solution.py:14
  38.5 7.3 %collective-permute-start.4 = (bf16[4,128,256]{2,1,0:T(8,128)(2,1)S(1)}, bf16[4,128,256]{2,1,0:T(8,128)(2,1)S(1)}, u32[]{:S(2)}, u32[]{:S(2)}) collective-permute-start(bf16[4,128,256]{2,1,0:T(8,128)(2,1)S(1)} %collective-permute-done.3), channel_id=1, source_target_pairs={{0,28},{4,0},{8,4},{12,8},{16,12},{20,16},{24,20},{28,24},{1,29},{... | collective-permute-start | bytes 786440 | tf_op jit(solution)/shard_map/ppermute | solution.py:14
  51.3 11.5 %copy-start.2 = (bf16[512,256]{1,0:T(8,128)(2,1)S(1)}, bf16[512,256]{1,0:T(8,128)(2,1)}, u32[]{:S(2)}) copy-start(bf16[512,256]{1,0:T(8,128)(2,1)} %param.19) | copy-start | bytes 786436
  51.3 10.6 %all-to-all-start.1 = ((bf16[4,2,128,256]{3,1,2,0:T(2,128)(2,1)}), bf16[4,2,128,256]{3,1,2,0:T(2,128)(2,1)S(1)}, u32[]{:S(2)}, u32[]{:S(2)}) async-start(bf16[4,2,128,256]{3,1,2,0:T(2,128)(2,1)} %copy.100), calls=%async_computation.1 | async-start | bytes 1048576 | tf_op jit(solution)/shard_map/all_to_all | solution.py:62
  65.7 10.0 %all-to-all-start.2 = ((bf16[4,2,128,256]{3,2,1,0:T(8,128)(2,1)}), bf16[4,2,128,256]{3,2,1,0:T(8,128)(2,1)S(1)}, u32[]{:S(2)}, u32[]{:S(2)}) async-start(bf16[4,2,128,256]{3,2,1,0:T(8,128)(2,1)} %broadcast_select_fusion), calls=%async_computation.2 | async-start | bytes 1048576 | tf_op jit(solution)/shard_map/all_to_all | solution.py:85
  69.2 180.8 %all-reduce.2.cloned.1.call-start = ((), (), s32[]{:S(2)}) async-start(), calls=%async_computation.3 | async-start | bytes 524288 | tf_op jit(solution)/shard_map/psum | solution.py:79
  77.2 10.5 %collective-permute-start.5 = (f32[4,128,256]{2,0,1:T(4,128)S(1)}, f32[4,128,256]{2,0,1:T(4,128)S(1)}, u32[]{:S(2)}, u32[]{:S(2)}) collective-permute-start(f32[4,128,256]{2,0,1:T(4,128)S(1)} %fusion.67), channel_id=1, source_target_pairs={{0,4},{4,8},{8,12},{12,16},{16,20},{20,24},{24,28},{28,0},{1,5},{5... | collective-permute-start | bytes 1572872 | tf_op jit(solution)/shard_map/ppermute | solution.py:14
  88.0 10.6 %collective-permute-start.6 = (f32[4,128,256]{2,0,1:T(4,128)S(1)}, f32[4,128,256]{2,0,1:T(4,128)}, u32[]{:S(2)}, u32[]{:S(2)}) collective-permute-start(f32[4,128,256]{2,0,1:T(4,128)S(1)} %convolution_add_fusion), channel_id=1, source_target_pairs={{0,4},{4,8},{8,12},{12,16},{16,20},{20,24},{24,28},{28,0},{1,5},{5... | collective-permute-start | bytes 1572872 | tf_op jit(solution)/shard_map/ppermute | solution.py:14
  99.7 10.6 %collective-permute-start.7 = (f32[4,128,256]{2,0,1:T(4,128)S(1)}, f32[4,128,256]{2,0,1:T(4,128)}, u32[]{:S(2)}, u32[]{:S(2)}) collective-permute-start(f32[4,128,256]{2,0,1:T(4,128)S(1)} %add.48), channel_id=1, source_target_pairs={{0,4},{4,8},{8,12},{12,16},{16,20},{20,24},{24,28},{28,0},{1,5},{5... | collective-permute-start | bytes 1572872 | tf_op jit(solution)/shard_map/ppermute | solution.py:14
  111.5 13.4 %collective-permute-start.8 = (f32[4,128,256]{2,0,1:T(4,128)S(1)}, f32[4,128,256]{2,0,1:T(4,128)S(1)}, u32[]{:S(2)}, u32[]{:S(2)}) collective-permute-start(f32[4,128,256]{2,0,1:T(4,128)S(1)} %add.49), channel_id=1, source_target_pairs={{0,4},{4,8},{8,12},{12,16},{16,20},{20,24},{24,28},{28,0},{1,5},{5... | collective-permute-start | bytes 1572872 | tf_op jit(solution)/shard_map/ppermute | solution.py:14
  125.0 6.4 %collective-permute-start.9 = (bf16[4,128,256]{2,0,1:T(4,128)(2,1)S(1)}, bf16[4,128,256]{2,0,1:T(4,128)(2,1)S(1)}, u32[]{:S(2)}, u32[]{:S(2)}) collective-permute-start(bf16[4,128,256]{2,0,1:T(4,128)(2,1)S(1)} %add.50), channel_id=1, source_target_pairs={{0,24},{4,28},{8,0},{12,4},{16,8},{20,12},{24,16},{28,20},{1,25},{... | collective-permute-start | bytes 786440 | tf_op jit(solution)/shard_map/ppermute | solution.py:14
Sparse Core Ops, SparseCore 0:
  126.2 123.7 all-reduce.1
where the time goes:
time: 259 us; the launch traced here: 258 us
  waiting for transfers between devices  182 us (70%)
  starting transfers between devices  25.8 us (10%)
  local copies, waits for them, and re-layouts  18 us (7%)
  between operations  14.6 us (6%)
  matrix products  13.2 us (5%)
  other arithmetic  5.06 us (2%)
    psum x1, waiting for transfers between devices, per_device(): weight_grad = lax.psum(local_grad, ('dom', 'rows'))  118 us
    ppermute x10, waiting for transfers between devices, shifted(): return lax.ppermute(value, axis, pairs)  51.3 us
    ppermute x10, starting transfers between devices, shifted(): return lax.ppermute(value, axis, pairs)  14.5 us
    all_to_all x1, waiting for transfers between devices, per_device(): lax.all_to_all(reply_blocks, 'rows', split_axis=0, concat_axis=0, tiled=T...  6.41 us
    all_to_all x1, waiting for transfers between devices, per_device(): lax.all_to_all(partials, 'rows', split_axis=0, concat_axis=0, tiled=True)  6.26 us
    dot_general x5, matrix products, per_device(): jnp.einsum('tij,tjf->tif', values[step_idx], tile_picked, preferred_eleme...  6.19 us
  transfers between devices with their start and end apart: 14, of which 12 were waited for; matrix products, arithmetic and copies ran while one was open for 8% of the time, Pallas kernels for 0%

commit v1 on v0

v1 whole, which is shorter than its diff:
```python
import functools

import jax
import jax.numpy as jnp
from jax import lax
from jax.experimental import pallas as pl
from jax.experimental.pallas import tpu as pltpu
from jax.sharding import PartitionSpec as P

MESH = pl.DeviceIdType.MESH
B = 128
LANES = 128
OWN, NEAR, FAR, MATE, PASSED = range(5)
f32 = jnp.float32
bf16 = jnp.bfloat16


def dot(a, b):
    return jnp.dot(a, b, preferred_element_type=f32)


def kernel(
    dom_count, row_count,
    feat_ref, weight_ref, tiles_ref, source_ref, slot_ref, block_ref, count_ref, cot_ref,
    act_out, grad_out, wg_out,
    tiles, weight, weight_t, cot, sums, sums_t, picked, acc,
    own0, near0, far0, mate0, passed0, own1, near1, far1, mate1, passed1,
    ids_send, ids_recv,
    part_send, part_recv, agg, pre, pre_grad, agg_grad,
    reply_send, back0, back1,
    g_own, g_send, g_recv,
    wg_local, wg_rows, wg_chunk, wg_dom, wg_own,
    load_sem, feat_ss, feat_rs, ids_ss, ids_rs, part_ss, part_rs, reply_ss, reply_rs,
    g_ss, g_rs, w1_ss, w1_rs, w2_ss, w2_rs, w3_ss, w3_rs, w4_ss, w4_rs, out_sem,
):
    d = lax.axis_index("dom")
    r = lax.axis_index("rows")
    parity = d % 2
    sigma = 1 - 2 * parity
    halves = feat_ref.shape[1] // LANES
    nblk = feat_ref.shape[0] // B
    tps = tiles_ref.shape[2]
    cap = block_ref.shape[1] // row_count
    nodes = nblk * B
    mate_dev = (d + sigma, r)
    up_dev = (lax.rem(d + 2 * sigma + dom_count, dom_count), r)
    down_dev = (lax.rem(d - 2 * sigma + dom_count, dom_count), r)
    steps = (2, 2 + 2 * sigma, 2 - 2 * sigma, 2 + sigma, 2 - sigma)
    feats = ((own0, near0, far0, mate0, passed0), (own1, near1, far1, mate1, passed1))
    backs = (back0, back1)

    def row_at(shift):
        return lax.rem(r + shift + row_count, row_count)

    def dom_at(shift):
        return lax.rem(d + shift + dom_count, dom_count)

    def remote(src, dst, ss, rs, device):
        return pltpu.make_async_remote_copy(
            src_ref=src, dst_ref=dst, send_sem=ss, recv_sem=rs, device_id=device, device_id_type=MESH
        )

    barrier = pltpu.get_barrier_semaphore()

    @pl.loop(1, dom_count)
    def _(j):
        pl.semaphore_signal(barrier, inc=1, device_id=(dom_at(j), r), device_id_type=MESH)

    @pl.loop(1, row_count)
    def _(j):
        pl.semaphore_signal(barrier, inc=1, device_id=(d, row_at(j)), device_id_type=MESH)

    loads = [
        pltpu.make_async_copy(tiles_ref.at[0], tiles, load_sem.at[0]),
        pltpu.make_async_copy(weight_ref, weight, load_sem.at[1]),
        pltpu.make_async_copy(cot_ref, cot, load_sem.at[2]),
    ]
    for h in range(halves):
        for b in range(nblk):
            loads.append(
                pltpu.make_async_copy(
                    feat_ref.at[pl.ds(b * B, B), pl.ds(h * LANES, LANES)],
                    feats[h][OWN].at[b],
                    load_sem.at[3 + h * nblk + b],
                )
            )
    for copy in loads:
        copy.start()
    for copy in loads[3:]:
        copy.wait()
    pl.semaphore_wait(barrier, dom_count + row_count - 2)

    def feat_copy(h, role):
        own = feats[h][OWN]
        if role == PASSED:
            src, device = feats[h][NEAR], mate_dev
        elif role == MATE:
            src, device = own, mate_dev
        elif role == FAR:
            src, device = own, up_dev
        else:
            src, device = own, down_dev
        return remote(src, feats[h][role], feat_ss.at[h, role], feat_rs.at[h, role], device)

    for h in range(halves):
        for role in (NEAR, FAR, MATE):
            feat_copy(h, role).start()

    @pl.loop(0, row_count)
    def _(q):
        for c in range(cap):
            ids_send[q, c] = jnp.full((8, LANES), block_ref[0, q * cap + c], jnp.int32)

    ids_recv[0] = ids_send[r]

    def ids_copy(j):
        return remote(ids_send.at[row_at(j)], ids_recv.at[j], ids_ss.at[j], ids_rs.at[j], (d, row_at(j)))

    @pl.loop(1, row_count)
    def _(j):
        ids_copy(j).start()

    for copy in loads[:3]:
        copy.wait()

    def live(role, t):
        return t < count_ref[0, steps[role]]

    @pl.loop(0, row_count)
    def _(q):
        for role in range(5):
            for c in range(cap):
                for t in range(tps):
                    hit = live(role, t) & (slot_ref[0, steps[role], t] == q * cap + c)
                    scale = jnp.where(hit, 1.0, 0.0).astype(f32)
                    tile = tiles[steps[role], t].astype(f32) * scale
                    sums[role, pl.ds(pl.multiple_of((q * cap + c) * B, B), B), t * B:(t + 1) * B] = tile.astype(bf16)

    for role in range(5):
        for t in range(tps):
            turned = tiles[steps[role], t].astype(f32).T
            for b in range(nblk):
                hit = live(role, t) & (source_ref[0, steps[role], t] == b)
                scale = jnp.where(hit, 1.0, 0.0).astype(f32)
                sums_t[role, b * B:(b + 1) * B, t * B:(t + 1) * B] = (turned * scale).astype(bf16)
    weight_t[...] = weight[...].astype(f32).T.astype(bf16)

    total = row_count * cap * B
    span = min(total, 1024)

    def add_role(h, role, first):
        for t in range(tps):
            index = jnp.where(live(role, t), source_ref[0, steps[role], t], 0)
            picked[t * B:(t + 1) * B, :] = feats[h][role][index]

        @pl.loop(0, total // span)
        def _(i):
            rows = pl.ds(pl.multiple_of(i * span, span), span)
            product = dot(sums[role, rows, :], picked[...])
            if first:
                acc[rows, :] = product
            else:
                acc[rows, :] += product

    def part_copy(h, j):
        return remote(
            part_send.at[h, row_at(j)], part_recv.at[h, j], part_ss.at[h, j], part_rs.at[h, j], (d, row_at(j))
        )

    for h in range(halves):
        add_role(h, OWN, True)
        feat_copy(h, NEAR).wait_recv()
        feat_copy(h, PASSED).start()
        feat_copy(h, MATE).wait_recv()
        add_role(h, MATE, False)
        add_role(h, NEAR, False)
        feat_copy(h, FAR).wait_recv()
        add_role(h, FAR, False)
        feat_copy(h, PASSED).wait_recv()
        add_role(h, PASSED, False)

        @pl.loop(0, row_count)
        def _(q):
            rows = pl.ds(pl.multiple_of(q * cap * B, cap * B), cap * B)
            part_send[h, q] = acc[rows, :].astype(bf16)

        @pl.loop(1, row_count)
        def _(j):
            part_copy(h, j).start()

        part_recv[h, 0] = part_send[h, r]

    @pl.loop(1, row_count)
    def _(j):
        ids_copy(j).wait()

    def is_block(j, c, b):
        return ids_recv[j, c][0:1, :] == b

    for h in range(halves):
        @pl.loop(1, row_count)
        def _(j):
            part_copy(h, j).wait_recv()

        for b in range(nblk):
            def gather(j, value):
                for c in range(cap):
                    term = part_recv[h, j, c * B:(c + 1) * B, :].astype(f32)
                    value = value + jnp.where(is_block(j, c, b), term, 0.0)
                return value

            value = lax.fori_loop(0, row_count, gather, jnp.zeros((B, LANES), f32), unroll=row_count <= 4)
            agg[h, b * B:(b + 1) * B, :] = value.astype(bf16)
        product = dot(agg[h], weight[h * LANES:(h + 1) * LANES, :])
        if h == 0:
            pre[...] = product
        else:
            pre[...] += product

    value = pre[...]
    sig = jax.nn.sigmoid(value)
    slope = sig * (1.0 + value * (1.0 - sig))
    pre_grad[...] = (cot[...].astype(f32) * slope).astype(bf16)

    def reply_copy(h, j):
        rows = pl.ds(pl.multiple_of(r * cap, cap), cap)
        return remote(
            reply_send.at[h, j], backs[h].at[rows], reply_ss.at[h, j], reply_rs.at[h, j], (d, row_at(-j))
        )

    for h in range(halves):
        product = dot(pre_grad[...], weight_t[:, h * LANES:(h + 1) * LANES])
        agg_grad[...] = product.astype(bf16)

        @pl.loop(0, row_count)
        def _(j):
            for c in range(cap):
                chosen = jnp.zeros((B, LANES), f32)
                for b in range(nblk):
                    chosen = jnp.where(is_block(j, c, b), agg_grad[b * B:(b + 1) * B, :].astype(f32), chosen)
                reply_send[h, j, c] = chosen.astype(bf16)

        @pl.loop(1, row_count)
        def _(j):
            reply_copy(h, j).start()

        backs[h][pl.ds(pl.multiple_of(r * cap, cap), cap)] = reply_send[h, 0]

    act_out[...] = (value * sig).astype(bf16)

    for h in range(halves):
        wg_local[h * LANES:(h + 1) * LANES, :] = lax.dot_general(
            agg[h], pre_grad[...], (((0,), (0,)), ((), ())), preferred_element_type=f32
        )
    chunk = wg_local.shape[0] // row_count

    def w1_copy(j):
        rows = pl.ds(pl.multiple_of(row_at(j) * chunk, chunk), chunk)
        return remote(wg_local.at[rows], wg_rows.at[j], w1_ss.at[j], w1_rs.at[j], (d, row_at(j)))

    @pl.loop(1, row_count)
    def _(j):
        w1_copy(j).start()

    def g_copy(h, role):
        device = {NEAR: up_dev, FAR: down_dev, MATE: mate_dev, PASSED: mate_dev}[role]
        return remote(g_send.at[h, role], g_recv.at[h, role], g_ss.at[h, role], g_rs.at[h, role], device)

    for h in range(halves):
        @pl.loop(1, row_count)
        def _(j):
            reply_copy(h, j).wait_recv()

        def source_terms(role):
            for t in range(tps):
                index = jnp.where(live(role, t), slot_ref[0, steps[role], t], 0)
                picked[t * B:(t + 1) * B, :] = backs[h][index]
            return dot(sums_t[role], picked[...])

        for role in (PASSED, FAR):
            g_send[h, role] = source_terms(role).astype(bf16)
            g_copy(h, role).start()
        near = source_terms(NEAR)
        g_copy(h, PASSED).wait_recv()
        g_send[h, NEAR] = (near + g_recv[h, PASSED].astype(f32)).astype(bf16)
        g_copy(h, NEAR).start()
        g_send[h, MATE] = source_terms(MATE).astype(bf16)
        g_copy(h, MATE).start()
        g_own[h] = source_terms(OWN)

    wg_chunk[...] = wg_local[pl.ds(pl.multiple_of(r * chunk, chunk), chunk), :]

    @pl.loop(1, row_count)
    def _(j):
        w1_copy(j).wait_recv()
        wg_chunk[...] += wg_rows[j]

    piece = chunk // dom_count
    scatter = piece * dom_count == chunk and piece % 8 == 0
    mine = pl.ds(pl.multiple_of(r * chunk, chunk), chunk)
    if scatter:
        def w2_copy(j):
            rows = pl.ds(pl.multiple_of(dom_at(j) * piece, piece), piece)
            return remote(wg_chunk.at[rows], wg_dom.at[j], w2_ss.at[j], w2_rs.at[j], (dom_at(j), r))

        @pl.loop(1, dom_count)
        def _(j):
            w2_copy(j).start()

        wg_own[...] = wg_chunk[pl.ds(pl.multiple_of(d * piece, piece), piece), :]

        @pl.loop(1, dom_count)
        def _(j):
            w2_copy(j).wait_recv()
            wg_own[...] += wg_dom[j]

        def w3_copy(j):
            rows = pl.ds(pl.multiple_of(r * chunk + d * piece, piece), piece)
            return remote(wg_own, wg_out.at[rows], w3_ss.at[j], w3_rs.at[j], (dom_at(j), r))

        @pl.loop(1, dom_count)
        def _(j):
            w3_copy(j).start()

        wg_out[pl.ds(pl.multiple_of(r * chunk + d * piece, piece), piece), :] = wg_own[...]

        @pl.loop(1, dom_count)
        def _(j):
            w3_copy(j).wait()
    else:
        def w2_copy(j):
            return remote(wg_chunk, wg_dom.at[d], w2_ss.at[j], w2_rs.at[j], (dom_at(j), r))

        @pl.loop(1, dom_count)
        def _(j):
            w2_copy(j).start()

        wg_dom[d] = wg_chunk[...]

        @pl.loop(1, dom_count)
        def _(j):
            w2_copy(j).wait_recv()

        wg_out[mine, :] = lax.fori_loop(
            0, dom_count, lambda i, value: value + wg_dom[i], jnp.zeros(wg_chunk.shape, f32)
        )

    def w4_copy(j):
        return remote(wg_out.at[mine], wg_out.at[mine], w4_ss.at[j], w4_rs.at[j], (d, row_at(j)))

    @pl.loop(1, row_count)
    def _(j):
        w4_copy(j).start()

    for h in range(halves):
        for role in (MATE, NEAR, FAR):
            g_copy(h, role).wait_recv()
        value = g_own[h]
        for role in (MATE, NEAR, FAR):
            value = value + g_recv[h, role].astype(f32)
        grad_out[:, h * LANES:(h + 1) * LANES] = value.astype(bf16)

    @pl.loop(1, row_count)
    def _(j):
        w4_copy(j).wait()

    for h in range(halves):
        for role in (NEAR, FAR, MATE, PASSED):
            feat_copy(h, role).wait_send()
            g_copy(h, role).wait_send()

        @pl.loop(1, row_count)
        def _(j):
            part_copy(h, j).wait_send()
            reply_copy(h, j).wait_send()

    @pl.loop(1, row_count)
    def _(j):
        w1_copy(j).wait_send()

    @pl.loop(1, dom_count)
    def _(j):
        w2_copy(j).wait_send()


def per_device(
    features, weight, tile_values, tile_source, tile_slot, slot_block, tile_count, cotangent, *, dom_count, row_count
):
    nodes, channels = features.shape
    nblk = nodes // B
    halves = channels // LANES
    tps = tile_values.shape[2]
    slots = slot_block.shape[1]
    cap = slots // row_count
    chunk = channels // row_count
    piece = chunk // dom_count
    scatter = piece * dom_count == chunk and piece % 8 == 0
    vmem = pl.BlockSpec(memory_space=pltpu.VMEM)
    smem = pl.BlockSpec(memory_space=pltpu.SMEM)
    anywhere = pl.BlockSpec(memory_space=pl.ANY)
    V = pltpu.VMEM
    dma = pltpu.SemaphoreType.DMA
    scratch = [
        V(tile_values.shape[1:], bf16), V(weight.shape, bf16), V(weight.shape[::-1], bf16), V(cotangent.shape, bf16),
        V((5, slots * B, tps * B), bf16), V((5, nodes, tps * B), bf16), V((tps * B, LANES), bf16),
        V((slots * B, LANES), f32),
        *[V((nblk, B, LANES), bf16) for _ in range(10)],
        V((row_count, cap, 8, LANES), jnp.int32), V((row_count, cap, 8, LANES), jnp.int32),
        V((halves, row_count, cap * B, LANES), bf16), V((halves, row_count, cap * B, LANES), bf16),
        V((halves, nodes, LANES), bf16), V((nodes, channels), f32), V((nodes, channels), bf16), V((nodes, LANES), bf16),
        V((halves, row_count, cap, B, LANES), bf16), V((slots, B, LANES), bf16), V((slots, B, LANES), bf16),
        V((halves, nodes, LANES), f32), V((halves, 5, nodes, LANES), bf16), V((halves, 5, nodes, LANES), bf16),
        V((channels, channels), f32), V((row_count, chunk, channels), f32), V((chunk, channels), f32),
        V((dom_count, piece if scatter else chunk, channels), f32), V((piece if scatter else 8, channels), f32),
        dma((3 + halves * nblk,)), dma((halves, 5)), dma((halves, 5)), dma((row_count,)), dma((row_count,)),
        dma((halves, row_count)), dma((halves, row_count)), dma((halves, row_count)), dma((halves, row_count)),
        dma((halves, 5)), dma((halves, 5)),
        dma((row_count,)), dma((row_count,)), dma((dom_count,)), dma((dom_count,)),
        dma((dom_count,)), dma((dom_count,)), dma((row_count,)), dma((row_count,)), dma((1,)),
    ]
    return pl.pallas_call(
        functools.partial(kernel, dom_count, row_count),
        out_shape=(
            jax.ShapeDtypeStruct((nodes, channels), bf16),
            jax.ShapeDtypeStruct((nodes, channels), bf16),
            jax.ShapeDtypeStruct((channels, channels), f32),
        ),
        in_specs=[anywhere, anywhere, anywhere, smem, smem, smem, smem, anywhere],
        out_specs=(vmem, vmem, vmem),
        scratch_shapes=scratch,
        compiler_params=pltpu.CompilerParams(
            collective_id=0, has_side_effects=True, vmem_limit_bytes=56 * 1024 * 1024
        ),
        name="graph_layer",
    )(features, weight, tile_values, tile_source, tile_slot, slot_block, tile_count, cotangent)


def solution(mesh):
    both = P(("dom", "rows"))
    return jax.shard_map(
        functools.partial(per_device, dom_count=mesh.shape["dom"], row_count=mesh.shape["rows"]),
        mesh=mesh,
        in_specs=(both, P(), both, both, both, both, both, both),
        out_specs=(both, both, P()),
        check_vma=False,
    )
```

time: 259 us -> 64.6 us (0.25)
  waiting for transfers between devices: 182 us -> 0 us
  Pallas kernels: 0 us -> 58.2 us
  starting transfers between devices: 25.8 us -> 0 us
  between operations: 14.6 us -> 0.66 us
  matrix products: 13.2 us -> 0 us
  local copies, waits for them, and re-layouts: 18 us -> 5.5 us
  other arithmetic: 5.06 us -> 0 us
    psum x1 -> x0, waiting for transfers between devices: 118 us -> none  [per_device(): weight_grad = lax.psum(local_grad, ('dom', 'rows'))]
    pallas_call x0 -> x1, Pallas kernels: none -> 58.2 us  [per_device(): pl.pallas_call(functools.partial(kernel, dom_count, row_count), out_shape...]
    ppermute x10 -> x0, waiting for transfers between devices: 51.3 us -> none  [shifted(): return lax.ppermute(value, axis, pairs)]
    ppermute x10 -> x0, starting transfers between devices: 14.5 us -> none  [shifted(): return lax.ppermute(value, axis, pairs)]
    dot_general x20 -> x0, matrix products: 13.2 us -> none  [the longest x5 6.19 us: per_device(): jnp.einsum('tij,tjf->tif', values[step_idx], tile_picked, preferred_eleme...]
    all_to_all x3 -> x0, waiting for transfers between devices: 12.7 us -> none  [the longest x1 6.41 us: per_device(): lax.all_to_all(reply_blocks, 'rows', split_axis=0, concat_axis=0, tiled=T...]
    all_to_all x3 -> x0, starting transfers between devices: 11.2 us -> none  [the longest x1 4.04 us: per_device(): lax.all_to_all(partials, 'rows', split_axis=0, concat_axis=0, tiled=True)]
    gather x11 -> x0, local copies, waits for them, and re-layouts: 6.21 us -> none  [the longest x5 2.82 us: source_terms(): picked = jnp.take(returned, slot_ids[step_idx], axis=0)]
  transfers between devices with their start and end apart: 14 -> 0, of which waited for: 12 -> 0; matrix products, arithmetic and copies ran while one was open for 8% -> 0% of each run, Pallas kernels for 0% -> 0%
where the time goes in v1:
time: 64.6 us; the launch traced here: 64.4 us
  Pallas kernels  58.2 us (90%)
  local copies, waits for them, and re-layouts  5.5 us (9%)
  between operations  0.66 us (1%)
    pallas_call x1, Pallas kernels, per_device(): pl.pallas_call(functools.partial(kernel, dom_count, row_count), out_shape...  58.2 us
    unnamed x11, local copies, waits for them, and re-layouts  5.5 us

profile of v1, /device:TPU:0, one launch (start us, length us, event | category | flops | bytes accessed | tf_op | source)
XLA Modules:
  0.0 64.4 jit_solution(2720153121643977371)
XLA Ops:
  0.6 0.0 copy-start.2
  0.6 1.4 %copy.11.source_ref = s32[1,5,4]{2,1,0:T(8,128)} copy(s32[1,5,4]{1,2,0:T(4,128)} %param.11) | data formatting | bytes 160 | tf_op args[3]
  2.0 0.0 copy-done.2
  2.0 0.7 %copy.12.slot_ref = s32[1,5,4]{2,1,0:T(8,128)} copy(s32[1,5,4]{1,2,0:T(4,128)S(1)} %copy-done.2) | data formatting | bytes 160 | tf_op args[4]
  2.7 58.2 %graph_layer.1 = (bf16[512,256]{1,0:T(8,128)(2,1)}, bf16[512,256]{1,0:T(8,128)(2,1)}, f32[256,256]{1,0:T(8,128)}) custom-call(bf16[512,256]{1,0:T(8,128)(2,1)} %feat_ref.1, bf16[256,256]{1,0:T(8,128)(2,1)} %weight_ref.1, bf16[1,5,4,128,128]{4,3,2,1,0:T(8,128)(2,1)} %tiles_ref.1, s32[1,5,4]{2,1,0:T(8,128)} %copy.11.source_ref, s32[1,5,4]{2,1,0:T(8,128)} %copy.12.slot_ref, ...), custom_call_target="tpu_custom_call" | custom-call | tf_op jit(solution)/shard_map/graph_layer/pallas_call | solution.py:421
  60.9 0.0 copy-start.1
  60.9 1.7 %copy.16 = bf16[512,256]{1,0:T(8,128)(2,1)} copy(bf16[512,256]{1,0:T(8,128)(2,1)} %get-tuple-element.6) | data formatting | bytes 524288
  62.6 0.0 copy-done.1
  62.6 0.0 copy-start
  62.6 0.7 %copy.17 = bf16[512,256]{1,0:T(8,128)(2,1)} copy(bf16[512,256]{1,0:T(8,128)(2,1)S(1)} %copy-done.1) | data formatting | bytes 524288
  63.3 0.3 copy-done
  63.6 0.7 %copy.18 = f32[256,256]{1,0:T(8,128)} copy(f32[256,256]{1,0:T(8,128)S(1)} %copy-done) | data formatting | bytes 524288
Async XLA Ops:
  0.6 1.4 %copy-start.2 = (s32[1,5,4]{1,2,0:T(4,128)S(1)}, s32[1,5,4]{1,2,0:T(4,128)}, u32[]{:S(2)}) copy-start(s32[1,5,4]{1,2,0:T(4,128)} %param.12) | copy-start | bytes 244
  60.9 1.7 %copy-start.1 = (bf16[512,256]{1,0:T(8,128)(2,1)S(1)}, bf16[512,256]{1,0:T(8,128)(2,1)}, u32[]{:S(2)}) copy-start(bf16[512,256]{1,0:T(8,128)(2,1)} %get-tuple-element.7) | copy-start | bytes 786436
  62.6 1.0 %copy-start = (f32[256,256]{1,0:T(8,128)S(1)}, f32[256,256]{1,0:T(8,128)}, u32[]{:S(2)}) copy-start(f32[256,256]{1,0:T(8,128)} %get-tuple-element.8) | copy-start | bytes 786436

commit v2 on v1

--- a/solution.py
+++ b/solution.py
@@ -29,7 +29,7 @@
     part_send, part_recv, agg, pre, pre_grad, agg_grad,
     reply_send, back0, back1,
     g_own, g_send, g_recv,
-    wg_local, wg_rows, wg_chunk, wg_dom, wg_own,
+    wg_local, wg_rows, wg_chunk, wg_dom, wg_mine, act, grad,
     load_sem, feat_ss, feat_rs, ids_ss, ids_rs, part_ss, part_rs, reply_ss, reply_rs,
     g_ss, g_rs, w1_ss, w1_rs, w2_ss, w2_rs, w3_ss, w3_rs, w4_ss, w4_rs, out_sem,
 ):
@@ -37,8 +37,8 @@
     r = lax.axis_index("rows")
     parity = d % 2
     sigma = 1 - 2 * parity
-    halves = feat_ref.shape[1] // LANES
-    nblk = feat_ref.shape[0] // B
+    halves = feat_ref.shape[2] // LANES
+    nblk = feat_ref.shape[0]
     tps = tiles_ref.shape[2]
     cap = block_ref.shape[1] // row_count
     nodes = nblk * B
@@ -70,28 +70,22 @@
     def _(j):
         pl.semaphore_signal(barrier, inc=1, device_id=(d, row_at(j)), device_id_type=MESH)
 
+    def columns(h):
+        return feat_ref.at[:, :, pl.ds(h * LANES, LANES)]
+
     loads = [
         pltpu.make_async_copy(tiles_ref.at[0], tiles, load_sem.at[0]),
         pltpu.make_async_copy(weight_ref, weight, load_sem.at[1]),
         pltpu.make_async_copy(cot_ref, cot, load_sem.at[2]),
     ]
     for h in range(halves):
-        for b in range(nblk):
-            loads.append(
-                pltpu.make_async_copy(
-                    feat_ref.at[pl.ds(b * B, B), pl.ds(h * LANES, LANES)],
-                    feats[h][OWN].at[b],
-                    load_sem.at[3 + h * nblk + b],
-                )
-            )
+        loads.append(pltpu.make_async_copy(columns(h), feats[h][OWN], load_sem.at[3 + h]))
     for copy in loads:
         copy.start()
-    for copy in loads[3:]:
-        copy.wait()
     pl.semaphore_wait(barrier, dom_count + row_count - 2)
 
     def feat_copy(h, role):
-        own = feats[h][OWN]
+        own = columns(h)
         if role == PASSED:
             src, device = feats[h][NEAR], mate_dev
         elif role == MATE:
@@ -120,7 +114,7 @@
     def _(j):
         ids_copy(j).start()
 
-    for copy in loads[:3]:
+    for copy in loads:
         copy.wait()
 
     def live(role, t):
@@ -131,7 +125,7 @@
         for role in range(5):
             for c in range(cap):
                 for t in range(tps):
-                    hit = live(role, t) & (slot_ref[0, steps[role], t] == q * cap + c)
+                    hit = live(role, t) & (slot_ref[0, t, steps[role]] == q * cap + c)
                     scale = jnp.where(hit, 1.0, 0.0).astype(f32)
                     tile = tiles[steps[role], t].astype(f32) * scale
                     sums[role, pl.ds(pl.multiple_of((q * cap + c) * B, B), B), t * B:(t + 1) * B] = tile.astype(bf16)
@@ -140,7 +134,7 @@
         for t in range(tps):
             turned = tiles[steps[role], t].astype(f32).T
             for b in range(nblk):
-                hit = live(role, t) & (source_ref[0, steps[role], t] == b)
+                hit = live(role, t) & (source_ref[0, t, steps[role]] == b)
                 scale = jnp.where(hit, 1.0, 0.0).astype(f32)
                 sums_t[role, b * B:(b + 1) * B, t * B:(t + 1) * B] = (turned * scale).astype(bf16)
     weight_t[...] = weight[...].astype(f32).T.astype(bf16)
@@ -148,10 +142,13 @@
     total = row_count * cap * B
     span = min(total, 1024)
 
+    def pick(h, role):
+        for t in range(tps):
+            index = jnp.where(live(role, t), source_ref[0, t, steps[role]], 0)
+            picked[t * B:(t + 1) * B, :] = feats[h][role][index]
+
     def add_role(h, role, first):
-        for t in range(tps):
-            index = jnp.where(live(role, t), source_ref[0, steps[role], t], 0)
-            picked[t * B:(t + 1) * B, :] = feats[h][role][index]
+        pick(h, role)
 
         @pl.loop(0, total // span)
         def _(i):
@@ -177,17 +174,18 @@
         feat_copy(h, FAR).wait_recv()
         add_role(h, FAR, False)
         feat_copy(h, PASSED).wait_recv()
-        add_role(h, PASSED, False)
-
-        @pl.loop(0, row_count)
-        def _(q):
+        pick(h, PASSED)
+
+        def finish(q):
             rows = pl.ds(pl.multiple_of(q * cap * B, cap * B), cap * B)
-            part_send[h, q] = acc[rows, :].astype(bf16)
-
-        @pl.loop(1, row_count)
-        def _(j):
+            part_send[h, q] = (acc[rows, :] + dot(sums[PASSED, rows, :], picked[...])).astype(bf16)
+
+        @pl.loop(1, row_count)
+        def _(j):
+            finish(row_at(j))
             part_copy(h, j).start()
 
+        finish(r)
         part_recv[h, 0] = part_send[h, r]
 
     @pl.loop(1, row_count)
@@ -232,8 +230,7 @@
         product = dot(pre_grad[...], weight_t[:, h * LANES:(h + 1) * LANES])
         agg_grad[...] = product.astype(bf16)
 
-        @pl.loop(0, row_count)
-        def _(j):
+        def reply(j):
             for c in range(cap):
                 chosen = jnp.zeros((B, LANES), f32)
                 for b in range(nblk):
@@ -242,11 +239,15 @@
 
         @pl.loop(1, row_count)
         def _(j):
+            reply(j)
             reply_copy(h, j).start()
 
+        reply(0)
         backs[h][pl.ds(pl.multiple_of(r * cap, cap), cap)] = reply_send[h, 0]
 
-    act_out[...] = (value * sig).astype(bf16)
+    act[...] = (value * sig).astype(bf16)
+    act_copy = pltpu.make_async_copy(act, act_out, out_sem.at[0])
+    act_copy.start()
 
     for h in range(halves):
         wg_local[h * LANES:(h + 1) * LANES, :] = lax.dot_general(
@@ -262,6 +263,39 @@
     def _(j):
         w1_copy(j).start()
 
+    piece = chunk // dom_count
+    scatter = piece * dom_count == chunk and piece % 8 == 0
+    part = pl.ds(pl.multiple_of(d * piece, piece), piece)
+
+    def w2_copy(j):
+        if scatter:
+            rows = pl.ds(pl.multiple_of(dom_at(j) * piece, piece), piece)
+            return remote(wg_chunk.at[rows], wg_dom.at[j], w2_ss.at[j], w2_rs.at[j], (dom_at(j), r))
+        return remote(wg_chunk, wg_dom.at[d], w2_ss.at[j], w2_rs.at[j], (dom_at(j), r))
+
+    def w3_copy(j):
+        return remote(wg_mine.at[part], wg_mine.at[part], w3_ss.at[j], w3_rs.at[j], (dom_at(j), r))
+
+    def w4_copy(j):
+        rows = wg_out.at[pl.ds(pl.multiple_of(r * chunk, chunk), chunk)]
+        return remote(wg_mine, rows, w4_ss.at[j], w4_rs.at[j], (d, row_at(j)))
+
+    wg_copy = pltpu.make_async_copy(
+        wg_mine, wg_out.at[pl.ds(pl.multiple_of(r * chunk, chunk), chunk)], out_sem.at[1 + halves]
+    )
+
+    def wg_second():
+        wg_chunk[...] = wg_local[pl.ds(pl.multiple_of(r * chunk, chunk), chunk), :]
+
+        @pl.loop(1, row_count)
+        def _(j):
+            w1_copy(j).wait_recv()
+            wg_chunk[...] += wg_rows[j]
+
+        @pl.loop(1, dom_count)
+        def _(j):
+            w2_copy(j).start()
+
     def g_copy(h, role):
         device = {NEAR: up_dev, FAR: down_dev, MATE: mate_dev, PASSED: mate_dev}[role]
         return remote(g_send.at[h, role], g_recv.at[h, role], g_ss.at[h, role], g_rs.at[h, role], device)
@@ -273,7 +307,7 @@
 
         def source_terms(role):
             for t in range(tps):
-                index = jnp.where(live(role, t), slot_ref[0, steps[role], t], 0)
+                index = jnp.where(live(role, t), slot_ref[0, t, steps[role]], 0)
                 picked[t * B:(t + 1) * B, :] = backs[h][index]
             return dot(sums_t[role], picked[...])
 
@@ -287,70 +321,42 @@
         g_send[h, MATE] = source_terms(MATE).astype(bf16)
         g_copy(h, MATE).start()
         g_own[h] = source_terms(OWN)
-
-    wg_chunk[...] = wg_local[pl.ds(pl.multiple_of(r * chunk, chunk), chunk), :]
-
-    @pl.loop(1, row_count)
-    def _(j):
-        w1_copy(j).wait_recv()
-        wg_chunk[...] += wg_rows[j]
-
-    piece = chunk // dom_count
-    scatter = piece * dom_count == chunk and piece % 8 == 0
-    mine = pl.ds(pl.multiple_of(r * chunk, chunk), chunk)
+        if h == 0:
+            wg_second()
+
     if scatter:
-        def w2_copy(j):
-            rows = pl.ds(pl.multiple_of(dom_at(j) * piece, piece), piece)
-            return remote(wg_chunk.at[rows], wg_dom.at[j], w2_ss.at[j], w2_rs.at[j], (dom_at(j), r))
+        total_own = wg_chunk[part, :]
+        for j in range(1, dom_count):
+            w2_copy(j).wait_recv()
+            total_own = total_own + wg_dom[j]
+        wg_mine[part, :] = total_own
 
         @pl.loop(1, dom_count)
         def _(j):
-            w2_copy(j).start()
-
-        wg_own[...] = wg_chunk[pl.ds(pl.multiple_of(d * piece, piece), piece), :]
-
-        @pl.loop(1, dom_count)
-        def _(j):
-            w2_copy(j).wait_recv()
-            wg_own[...] += wg_dom[j]
-
-        def w3_copy(j):
-            rows = pl.ds(pl.multiple_of(r * chunk + d * piece, piece), piece)
-            return remote(wg_own, wg_out.at[rows], w3_ss.at[j], w3_rs.at[j], (dom_at(j), r))
-
-        @pl.loop(1, dom_count)
-        def _(j):
             w3_copy(j).start()
-
-        wg_out[pl.ds(pl.multiple_of(r * chunk + d * piece, piece), piece), :] = wg_own[...]
 
         @pl.loop(1, dom_count)
         def _(j):
             w3_copy(j).wait()
     else:
-        def w2_copy(j):
-            return remote(wg_chunk, wg_dom.at[d], w2_ss.at[j], w2_rs.at[j], (dom_at(j), r))
+        wg_dom[d] = wg_chunk[...]
 
         @pl.loop(1, dom_count)
         def _(j):
-            w2_copy(j).start()
-
-        wg_dom[d] = wg_chunk[...]
-
-        @pl.loop(1, dom_count)
-        def _(j):
             w2_copy(j).wait_recv()
 
-        wg_out[mine, :] = lax.fori_loop(
+        wg_mine[...] = lax.fori_loop(
             0, dom_count, lambda i, value: value + wg_dom[i], jnp.zeros(wg_chunk.shape, f32)
         )
 
-    def w4_copy(j):
-        return remote(wg_out.at[mine], wg_out.at[mine], w4_ss.at[j], w4_rs.at[j], (d, row_at(j)))
-
     @pl.loop(1, row_count)
     def _(j):
         w4_copy(j).start()
+
+    wg_copy.start()
+
+    def grad_copy(h):
+        return pltpu.make_async_copy(grad.at[h], grad_out.at[:, pl.ds(h * LANES, LANES)], out_sem.at[1 + h])
 
     for h in range(halves):
         for role in (MATE, NEAR, FAR):
@@ -358,16 +364,20 @@
         value = g_own[h]
         for role in (MATE, NEAR, FAR):
             value = value + g_recv[h, role].astype(f32)
-        grad_out[:, h * LANES:(h + 1) * LANES] = value.astype(bf16)
+        grad[h] = value.astype(bf16)
+        grad_copy(h).start()
 
     @pl.loop(1, row_count)
     def _(j):
         w4_copy(j).wait()
 
+    act_copy.wait()
+    wg_copy.wait()
     for h in range(halves):
         for role in (NEAR, FAR, MATE, PASSED):
             feat_copy(h, role).wait_send()
             g_copy(h, role).wait_send()
+        grad_copy(h).wait()
 
         @pl.loop(1, row_count)
         def _(j):
@@ -381,6 +391,14 @@
     @pl.loop(1, dom_count)
     def _(j):
         w2_copy(j).wait_send()
+
+
+def hand_over(a, b, c, to_a, to_b, to_c, sem):
+    copies = [pltpu.make_async_copy(x, y, sem.at[i]) for i, (x, y) in enumerate(((a, to_a), (b, to_b), (c, to_c)))]
+    for copy in copies:
+        copy.start()
+    for copy in copies:
+        copy.wait()
 
 
 def per_device(
@@ -395,7 +413,6 @@
     chunk = channels // row_count
     piece = chunk // dom_count
     scatter = piece * dom_count == chunk and piece % 8 == 0
-    vmem = pl.BlockSpec(memory_space=pltpu.VMEM)
     smem = pl.BlockSpec(memory_space=pltpu.SMEM)
     anywhere = pl.BlockSpec(memory_space=pl.ANY)
     V = pltpu.VMEM
@@ -411,14 +428,15 @@
         V((halves, row_count, cap, B, LANES), bf16), V((slots, B, LANES), bf16), V((slots, B, LANES), bf16),
         V((halves, nodes, LANES), f32), V((halves, 5, nodes, LANES), bf16), V((halves, 5, nodes, LANES), bf16),
         V((channels, channels), f32), V((row_count, chunk, channels), f32), V((chunk, channels), f32),
-        V((dom_count, piece if scatter else chunk, channels), f32), V((piece if scatter else 8, channels), f32),
-        dma((3 + halves * nblk,)), dma((halves, 5)), dma((halves, 5)), dma((row_count,)), dma((row_count,)),
+        V((dom_count, piece if scatter else chunk, channels), f32), V((chunk, channels), f32),
+        V((nodes, channels), bf16), V((halves, nodes, LANES), bf16),
+        dma((3 + halves,)), dma((halves, 5)), dma((halves, 5)), dma((row_count,)), dma((row_count,)),
         dma((halves, row_count)), dma((halves, row_count)), dma((halves, row_count)), dma((halves, row_count)),
         dma((halves, 5)), dma((halves, 5)),
         dma((row_count,)), dma((row_count,)), dma((dom_count,)), dma((dom_count,)),
-        dma((dom_count,)), dma((dom_count,)), dma((row_count,)), dma((row_count,)), dma((1,)),
+        dma((dom_count,)), dma((dom_count,)), dma((row_count,)), dma((row_count,)), dma((2 + halves,)),
     ]
-    return pl.pallas_call(
+    results = pl.pallas_call(
         functools.partial(kernel, dom_count, row_count),
         out_shape=(
             jax.ShapeDtypeStruct((nodes, channels), bf16),
@@ -426,13 +444,25 @@
             jax.ShapeDtypeStruct((channels, channels), f32),
         ),
         in_specs=[anywhere, anywhere, anywhere, smem, smem, smem, smem, anywhere],
-        out_specs=(vmem, vmem, vmem),
+        out_specs=(anywhere, anywhere, anywhere),
         scratch_shapes=scratch,
         compiler_params=pltpu.CompilerParams(
             collective_id=0, has_side_effects=True, vmem_limit_bytes=56 * 1024 * 1024
         ),
         name="graph_layer",
-    )(features, weight, tile_values, tile_source, tile_slot, slot_block, tile_count, cotangent)
+    )(
+        features.reshape(nblk, B, channels), weight, tile_values,
+        jnp.swapaxes(tile_source, 1, 2), jnp.swapaxes(tile_slot, 1, 2), slot_block, tile_count, cotangent,
+    )
+    return pl.pallas_call(
+        hand_over,
+        out_shape=tuple(jax.ShapeDtypeStruct(x.shape, x.dtype) for x in results),
+        in_specs=[anywhere] * 3,
+        out_specs=(anywhere,) * 3,
+        scratch_shapes=[dma((3,))],
+        compiler_params=pltpu.CompilerParams(vmem_limit_bytes=60 * 1024 * 1024),
+        name="hand_over",
+    )(*results)
 
 
 def solution(mesh):

time: 64.6 us -> 80.6 us (1.25)
  Pallas kernels: 58.2 us -> 79.8 us
  local copies, waits for them, and re-layouts: 5.5 us -> 0 us
    pallas_call x0 -> x1, Pallas kernels: none -> 25 us  [per_device(): pl.pallas_call(hand_over, out_shape=tuple((jax.ShapeDtypeStruct(x.shape,...]
    unnamed x11 -> x0, local copies, waits for them, and re-layouts: 5.5 us -> none
    pallas_call x1, Pallas kernels: 58.2 us -> 54.8 us  [per_device(): pl.pallas_call(functools.partial(kernel, dom_count, row_count), out_shape...]
where the time goes in v2:
time: 80.6 us; the launch traced here: 80.4 us
  Pallas kernels  79.8 us (99%)
    pallas_call x1, Pallas kernels, per_device(): pl.pallas_call(functools.partial(kernel, dom_count, row_count), out_shape...  54.8 us
    pallas_call x1, Pallas kernels, per_device(): pl.pallas_call(hand_over, out_shape=tuple((jax.ShapeDtypeStruct(x.shape,...  25 us

profile of v2, /device:TPU:0, one launch (start us, length us, event | category | flops | bytes accessed | tf_op | source)
XLA Modules:
  0.0 80.4 jit_solution(7723037254402740220)
XLA Ops:
  0.6 54.8 %graph_layer.1 = (bf16[512,256]{1,0:T(8,128)(2,1)}, bf16[512,256]{1,0:T(8,128)(2,1)}, f32[256,256]{1,0:T(8,128)}) custom-call(bf16[4,128,256]{2,1,0:T(8,128)(2,1)} %bitcast.3, bf16[256,256]{1,0:T(8,128)(2,1)} %weight_ref.1, bf16[1,5,4,128,128]{4,3,2,1,0:T(8,128)(2,1)} %tiles_ref.1, s32[1,4,5]{2,1,0:T(4,128)} %bitcast.4, s32[1,4,5]{2,1,0:T(4,128)} %bitcast.5, ...), custom_call_target="tpu_custom_call" | custom-call | tf_op jit(solution)/shard_map/graph_layer/pallas_call | solution.py:439
  55.5 25.0 %hand_over.1 = (bf16[512,256]{1,0:T(8,128)(2,1)}, bf16[512,256]{1,0:T(8,128)(2,1)}, f32[256,256]{1,0:T(8,128)}) custom-call(bf16[512,256]{1,0:T(8,128)(2,1)} %get-tuple-element.6.a, bf16[512,256]{1,0:T(8,128)(2,1)} %get-tuple-element.7.b, f32[256,256]{1,0:T(8,128)} %get-tuple-element.8.c), custom_call_target="tpu_custom_call" | custom-call | tf_op jit(solution)/shard_map/hand_over/pallas_call | solution.py:457

commit v3 on v2

--- a/solution.py
+++ b/solution.py
@@ -276,9 +276,17 @@
     def w3_copy(j):
         return remote(wg_mine.at[part], wg_mine.at[part], w3_ss.at[j], w3_rs.at[j], (dom_at(j), r))
 
-    def w4_copy(j):
-        rows = wg_out.at[pl.ds(pl.multiple_of(r * chunk, chunk), chunk)]
-        return remote(wg_mine, rows, w4_ss.at[j], w4_rs.at[j], (d, row_at(j)))
+    def w4_copy(i, j):
+        span = piece if scatter else chunk
+        start = dom_at(-i) * piece if scatter else 0
+        src = wg_mine.at[pl.ds(pl.multiple_of(start, span), span)]
+        dst = wg_out.at[pl.ds(pl.multiple_of(r * chunk + start, span), span)]
+        return remote(src, dst, w4_ss.at[i, j], w4_rs.at[i, j], (d, row_at(j)))
+
+    def w4_start(i):
+        @pl.loop(1, row_count)
+        def _(j):
+            w4_copy(i, j).start()
 
     wg_copy = pltpu.make_async_copy(
         wg_mine, wg_out.at[pl.ds(pl.multiple_of(r * chunk, chunk), chunk)], out_sem.at[1 + halves]
@@ -335,9 +343,16 @@
         def _(j):
             w3_copy(j).start()
 
+        w4_start(0)
+
         @pl.loop(1, dom_count)
         def _(j):
-            w3_copy(j).wait()
+            w3_copy(j).wait_recv()
+            w4_start(j)
+
+        @pl.loop(1, dom_count)
+        def _(j):
+            w3_copy(j).wait_send()
     else:
         wg_dom[d] = wg_chunk[...]
 
@@ -349,9 +364,7 @@
             0, dom_count, lambda i, value: value + wg_dom[i], jnp.zeros(wg_chunk.shape, f32)
         )
 
-    @pl.loop(1, row_count)
-    def _(j):
-        w4_copy(j).start()
+        w4_start(0)
 
     wg_copy.start()
 
@@ -367,9 +380,11 @@
         grad[h] = value.astype(bf16)
         grad_copy(h).start()
 
-    @pl.loop(1, row_count)
-    def _(j):
-        w4_copy(j).wait()
+    @pl.loop(0, dom_count if scatter else 1)
+    def _(i):
+        @pl.loop(1, row_count)
+        def _(j):
+            w4_copy(i, j).wait()
 
     act_copy.wait()
     wg_copy.wait()
@@ -393,11 +408,16 @@
         w2_copy(j).wait_send()
 
 
-def hand_over(a, b, c, to_a, to_b, to_c, sem):
-    copies = [pltpu.make_async_copy(x, y, sem.at[i]) for i, (x, y) in enumerate(((a, to_a), (b, to_b), (c, to_c)))]
-    for copy in copies:
+def hand_over(a, b, c, to_a, to_b, to_c, in_a, in_b, in_c, sem):
+    triples = ((a, in_a, to_a), (b, in_b, to_b), (c, in_c, to_c))
+    reads = [pltpu.make_async_copy(x, y, sem.at[0, i]) for i, (x, y, _) in enumerate(triples)]
+    writes = [pltpu.make_async_copy(y, z, sem.at[1, i]) for i, (_, y, z) in enumerate(triples)]
+    for copy in reads:
         copy.start()
-    for copy in copies:
+    for read, write in zip(reads, writes):
+        read.wait()
+        write.start()
+    for copy in writes:
         copy.wait()
 
 
@@ -434,7 +454,7 @@
         dma((halves, row_count)), dma((halves, row_count)), dma((halves, row_count)), dma((halves, row_count)),
         dma((halves, 5)), dma((halves, 5)),
         dma((row_count,)), dma((row_count,)), dma((dom_count,)), dma((dom_count,)),
-        dma((dom_count,)), dma((dom_count,)), dma((row_count,)), dma((row_count,)), dma((2 + halves,)),
+        dma((dom_count,)), dma((dom_count,)), dma((dom_count, row_count)), dma((dom_count, row_count)), dma((2 + halves,)),
     ]
     results = pl.pallas_call(
         functools.partial(kernel, dom_count, row_count),
@@ -459,7 +479,7 @@
         out_shape=tuple(jax.ShapeDtypeStruct(x.shape, x.dtype) for x in results),
         in_specs=[anywhere] * 3,
         out_specs=(anywhere,) * 3,
-        scratch_shapes=[dma((3,))],
+        scratch_shapes=[*[V(x.shape, x.dtype) for x in results], dma((2, 3))],
         compiler_params=pltpu.CompilerParams(vmem_limit_bytes=60 * 1024 * 1024),
         name="hand_over",
     )(*results)

time: 80.6 us -> 57.4 us (0.71)
  Pallas kernels: 79.8 us -> 56.6 us
    pallas_call x1, Pallas kernels: 25 us -> 1.88 us  [per_device(): pl.pallas_call(hand_over, out_shape=tuple((jax.ShapeDtypeStruct(x.shape,...]
where the time goes in v3:
time: 57.4 us; the launch traced here: 57.2 us
  Pallas kernels  56.6 us (99%)
  between operations  0.64 us (1%)
    pallas_call x1, Pallas kernels, per_device(): pl.pallas_call(functools.partial(kernel, dom_count, row_count), out_shape...  54.7 us
    pallas_call x1, Pallas kernels, per_device(): pl.pallas_call(hand_over, out_shape=tuple((jax.ShapeDtypeStruct(x.shape,...  1.88 us

profile of v3, /device:TPU:0, one launch (start us, length us, event | category | flops | bytes accessed | tf_op | source)
XLA Modules:
  0.0 57.2 jit_solution(3412831874595713690)
XLA Ops:
  0.6 54.7 %graph_layer.1 = (bf16[512,256]{1,0:T(8,128)(2,1)}, bf16[512,256]{1,0:T(8,128)(2,1)}, f32[256,256]{1,0:T(8,128)}) custom-call(bf16[4,128,256]{2,1,0:T(8,128)(2,1)} %bitcast.3, bf16[256,256]{1,0:T(8,128)(2,1)} %weight_ref.1, bf16[1,5,4,128,128]{4,3,2,1,0:T(8,128)(2,1)} %tiles_ref.1, s32[1,4,5]{2,1,0:T(4,128)} %bitcast.4, s32[1,4,5]{2,1,0:T(4,128)} %bitcast.5, ...), custom_call_target="tpu_custom_call" | custom-call | tf_op jit(solution)/shard_map/graph_layer/pallas_call | solution.py:459
  55.3 1.9 %hand_over.1 = (bf16[512,256]{1,0:T(8,128)(2,1)}, bf16[512,256]{1,0:T(8,128)(2,1)}, f32[256,256]{1,0:T(8,128)}) custom-call(bf16[512,256]{1,0:T(8,128)(2,1)} %get-tuple-element.6.a, bf16[512,256]{1,0:T(8,128)(2,1)} %get-tuple-element.7.b, f32[256,256]{1,0:T(8,128)} %get-tuple-element.8.c), custom_call_target="tpu_custom_call" | custom-call | tf_op jit(solution)/shard_map/hand_over/pallas_call | solution.py:477

commit v4 on v3

--- a/solution.py
+++ b/solution.py
@@ -96,9 +96,8 @@
             src, device = own, down_dev
         return remote(src, feats[h][role], feat_ss.at[h, role], feat_rs.at[h, role], device)
 
-    for h in range(halves):
-        for role in (NEAR, FAR, MATE):
-            feat_copy(h, role).start()
+    for role in (NEAR, FAR, MATE):
+        feat_copy(0, role).start()
 
     @pl.loop(0, row_count)
     def _(q):
@@ -138,6 +137,12 @@
                 scale = jnp.where(hit, 1.0, 0.0).astype(f32)
                 sums_t[role, b * B:(b + 1) * B, t * B:(t + 1) * B] = (turned * scale).astype(bf16)
     weight_t[...] = weight[...].astype(f32).T.astype(bf16)
+
+    for h in range(1, halves):
+        for role in (NEAR, FAR):
+            feat_copy(h - 1, role).wait_send()
+        for role in (NEAR, FAR, MATE):
+            feat_copy(h, role).start()
 
     total = row_count * cap * B
     span = min(total, 1024)
@@ -390,7 +395,8 @@
     wg_copy.wait()
     for h in range(halves):
         for role in (NEAR, FAR, MATE, PASSED):
-            feat_copy(h, role).wait_send()
+            if h == halves - 1 or role in (MATE, PASSED):
+                feat_copy(h, role).wait_send()
             g_copy(h, role).wait_send()
         grad_copy(h).wait()
 

time: 57.4 us -> 57.2 us (level)
  no operation moved by 1% of the time
where the time goes in v4:
time: 57.2 us; the launch traced here: 57 us
  Pallas kernels  56.4 us (99%)
  between operations  0.64 us (1%)
    pallas_call x1, Pallas kernels, per_device(): pl.pallas_call(functools.partial(kernel, dom_count, row_count), out_shape...  54.5 us
    pallas_call x1, Pallas kernels, per_device(): pl.pallas_call(hand_over, out_shape=tuple((jax.ShapeDtypeStruct(x.shape,...  1.88 us

profile of v4, /device:TPU:0, one launch (start us, length us, event | category | flops | bytes accessed | tf_op | source)
XLA Modules:
  0.0 57.0 jit_solution(11407503322255912688)
XLA Ops:
  0.6 54.5 %graph_layer.1 = (bf16[512,256]{1,0:T(8,128)(2,1)}, bf16[512,256]{1,0:T(8,128)(2,1)}, f32[256,256]{1,0:T(8,128)}) custom-call(bf16[4,128,256]{2,1,0:T(8,128)(2,1)} %bitcast.3, bf16[256,256]{1,0:T(8,128)(2,1)} %weight_ref.1, bf16[1,5,4,128,128]{4,3,2,1,0:T(8,128)(2,1)} %tiles_ref.1, s32[1,4,5]{2,1,0:T(4,128)} %bitcast.4, s32[1,4,5]{2,1,0:T(4,128)} %bitcast.5, ...), custom_call_target="tpu_custom_call" | custom-call | tf_op jit(solution)/shard_map/graph_layer/pallas_call | solution.py:465
  55.1 1.9 %hand_over.1 = (bf16[512,256]{1,0:T(8,128)(2,1)}, bf16[512,256]{1,0:T(8,128)(2,1)}, f32[256,256]{1,0:T(8,128)}) custom-call(bf16[512,256]{1,0:T(8,128)(2,1)} %get-tuple-element.6.a, bf16[512,256]{1,0:T(8,128)(2,1)} %get-tuple-element.7.b, f32[256,256]{1,0:T(8,128)} %get-tuple-element.8.c), custom_call_target="tpu_custom_call" | custom-call | tf_op jit(solution)/shard_map/hand_over/pallas_call | solution.py:483

commit v5 on v3

--- a/solution.py
+++ b/solution.py
@@ -23,7 +23,7 @@
     dom_count, row_count,
     feat_ref, weight_ref, tiles_ref, source_ref, slot_ref, block_ref, count_ref, cot_ref,
     act_out, grad_out, wg_out,
-    tiles, weight, weight_t, cot, sums, sums_t, picked, acc,
+    tiles, tiles_t, weight, weight_t, cot, prod, acc,
     own0, near0, far0, mate0, passed0, own1, near1, far1, mate1, passed1,
     ids_send, ids_recv,
     part_send, part_recv, agg, pre, pre_grad, agg_grad,
@@ -120,44 +120,33 @@
     def live(role, t):
         return t < count_ref[0, steps[role]]
 
-    @pl.loop(0, row_count)
-    def _(q):
-        for role in range(5):
-            for c in range(cap):
-                for t in range(tps):
-                    hit = live(role, t) & (slot_ref[0, t, steps[role]] == q * cap + c)
-                    scale = jnp.where(hit, 1.0, 0.0).astype(f32)
-                    tile = tiles[steps[role], t].astype(f32) * scale
-                    sums[role, pl.ds(pl.multiple_of((q * cap + c) * B, B), B), t * B:(t + 1) * B] = tile.astype(bf16)
-
-    for role in range(5):
+    @pl.loop(0, tiles.shape[0])
+    def _(k):
         for t in range(tps):
-            turned = tiles[steps[role], t].astype(f32).T
-            for b in range(nblk):
-                hit = live(role, t) & (source_ref[0, t, steps[role]] == b)
-                scale = jnp.where(hit, 1.0, 0.0).astype(f32)
-                sums_t[role, b * B:(b + 1) * B, t * B:(t + 1) * B] = (turned * scale).astype(bf16)
+            tiles_t[k, t] = tiles[k, t].astype(f32).T.astype(bf16)
+
     weight_t[...] = weight[...].astype(f32).T.astype(bf16)
 
-    total = row_count * cap * B
-    span = min(total, 1024)
-
-    def pick(h, role):
+    def products(matrices, blocks, index_ref, role):
         for t in range(tps):
-            index = jnp.where(live(role, t), source_ref[0, t, steps[role]], 0)
-            picked[t * B:(t + 1) * B, :] = feats[h][role][index]
+            index = jnp.where(live(role, t), index_ref[0, t, steps[role]], 0)
+            prod[t] = dot(matrices[steps[role], t], blocks[index])
+
+    def mixed(index_ref, role, wanted):
+        value = None
+        for t in range(tps):
+            hit = live(role, t) & (index_ref[0, t, steps[role]] == wanted)
+            term = prod[t] * jnp.where(hit, 1.0, 0.0).astype(f32)
+            value = term if value is None else value + term
+        return value
 
     def add_role(h, role, first):
-        pick(h, role)
-
-        @pl.loop(0, total // span)
-        def _(i):
-            rows = pl.ds(pl.multiple_of(i * span, span), span)
-            product = dot(sums[role, rows, :], picked[...])
-            if first:
-                acc[rows, :] = product
-            else:
-                acc[rows, :] += product
+        products(tiles, feats[h][role], source_ref, role)
+
+        @pl.loop(0, row_count * cap)
+        def _(slot):
+            value = mixed(slot_ref, role, slot)
+            acc[slot] = value if first else acc[slot] + value
 
     def part_copy(h, j):
         return remote(
@@ -174,11 +163,12 @@
         feat_copy(h, FAR).wait_recv()
         add_role(h, FAR, False)
         feat_copy(h, PASSED).wait_recv()
-        pick(h, PASSED)
+        products(tiles, feats[h][PASSED], source_ref, PASSED)
 
         def finish(q):
-            rows = pl.ds(pl.multiple_of(q * cap * B, cap * B), cap * B)
-            part_send[h, q] = (acc[rows, :] + dot(sums[PASSED, rows, :], picked[...])).astype(bf16)
+            for c in range(cap):
+                value = acc[q * cap + c] + mixed(slot_ref, PASSED, q * cap + c)
+                part_send[h, q, c * B:(c + 1) * B, :] = value.astype(bf16)
 
         @pl.loop(1, row_count)
         def _(j):
@@ -200,7 +190,8 @@
         def _(j):
             part_copy(h, j).wait_recv()
 
-        for b in range(nblk):
+        @pl.loop(0, nblk)
+        def _(b):
             def gather(j, value):
                 for c in range(cap):
                     term = part_recv[h, j, c * B:(c + 1) * B, :].astype(f32)
@@ -208,17 +199,20 @@
                 return value
 
             value = lax.fori_loop(0, row_count, gather, jnp.zeros((B, LANES), f32), unroll=row_count <= 4)
-            agg[h, b * B:(b + 1) * B, :] = value.astype(bf16)
-        product = dot(agg[h], weight[h * LANES:(h + 1) * LANES, :])
-        if h == 0:
-            pre[...] = product
-        else:
-            pre[...] += product
-
-    value = pre[...]
-    sig = jax.nn.sigmoid(value)
-    slope = sig * (1.0 + value * (1.0 - sig))
-    pre_grad[...] = (cot[...].astype(f32) * slope).astype(bf16)
+            rows = pl.ds(pl.multiple_of(b * B, B), B)
+            agg[h, rows, :] = value.astype(bf16)
+            product = dot(value.astype(bf16), weight[h * LANES:(h + 1) * LANES, :])
+            if h > 0:
+                product = pre[rows, :] + product
+            pre[rows, :] = product
+            if h == halves - 1:
+                sig = jax.nn.sigmoid(product)
+                slope = sig * (1.0 + product * (1.0 - sig))
+                pre_grad[rows, :] = (cot[rows, :].astype(f32) * slope).astype(bf16)
+                act[rows, :] = (product * sig).astype(bf16)
+
+    act_copy = pltpu.make_async_copy(act, act_out, out_sem.at[0])
+    act_copy.start()
 
     def reply_copy(h, j):
         rows = pl.ds(pl.multiple_of(r * cap, cap), cap)
@@ -245,9 +239,6 @@
         reply(0)
         backs[h][pl.ds(pl.multiple_of(r * cap, cap), cap)] = reply_send[h, 0]
 
-    act[...] = (value * sig).astype(bf16)
-    act_copy = pltpu.make_async_copy(act, act_out, out_sem.at[0])
-    act_copy.start()
 
     for h in range(halves):
         wg_local[h * LANES:(h + 1) * LANES, :] = lax.dot_general(
@@ -313,22 +304,26 @@
         def _(j):
             reply_copy(h, j).wait_recv()
 
-        def source_terms(role):
-            for t in range(tps):
-                index = jnp.where(live(role, t), slot_ref[0, t, steps[role]], 0)
-                picked[t * B:(t + 1) * B, :] = backs[h][index]
-            return dot(sums_t[role], picked[...])
+        def source_terms(role, target, extra=None):
+            products(tiles_t, backs[h], slot_ref, role)
+
+            @pl.loop(0, nblk)
+            def _(b):
+                rows = pl.ds(pl.multiple_of(b * B, B), B)
+                value = mixed(source_ref, role, b)
+                if extra is not None:
+                    value = value + extra[rows, :].astype(f32)
+                target[rows, :] = value.astype(target.dtype)
 
         for role in (PASSED, FAR):
-            g_send[h, role] = source_terms(role).astype(bf16)
+            source_terms(role, g_send.at[h, role])
             g_copy(h, role).start()
-        near = source_terms(NEAR)
         g_copy(h, PASSED).wait_recv()
-        g_send[h, NEAR] = (near + g_recv[h, PASSED].astype(f32)).astype(bf16)
+        source_terms(NEAR, g_send.at[h, NEAR], g_recv.at[h, PASSED])
         g_copy(h, NEAR).start()
-        g_send[h, MATE] = source_terms(MATE).astype(bf16)
+        source_terms(MATE, g_send.at[h, MATE])
         g_copy(h, MATE).start()
-        g_own[h] = source_terms(OWN)
+        source_terms(OWN, g_own.at[h])
         if h == 0:
             wg_second()
 
@@ -438,9 +433,8 @@
     V = pltpu.VMEM
     dma = pltpu.SemaphoreType.DMA
     scratch = [
-        V(tile_values.shape[1:], bf16), V(weight.shape, bf16), V(weight.shape[::-1], bf16), V(cotangent.shape, bf16),
-        V((5, slots * B, tps * B), bf16), V((5, nodes, tps * B), bf16), V((tps * B, LANES), bf16),
-        V((slots * B, LANES), f32),
+        V(tile_values.shape[1:], bf16), V(tile_values.shape[1:], bf16), V(weight.shape, bf16), V(weight.shape[::-1], bf16), V(cotangent.shape, bf16),
+        V((tps, B, LANES), f32), V((slots, B, LANES), f32),
         *[V((nblk, B, LANES), bf16) for _ in range(10)],
         V((row_count, cap, 8, LANES), jnp.int32), V((row_count, cap, 8, LANES), jnp.int32),
         V((halves, row_count, cap * B, LANES), bf16), V((halves, row_count, cap * B, LANES), bf16),

time: 57.4 us -> 57.3 us (level)
  no operation moved by 1% of the time
where the time goes in v5:
time: 57.3 us; the launch traced here: 57.1 us
  Pallas kernels  56.5 us (99%)
  between operations  0.64 us (1%)
    pallas_call x1, Pallas kernels, per_device(): pl.pallas_call(functools.partial(kernel, dom_count, row_count), out_shape...  54.6 us
    pallas_call x1, Pallas kernels, per_device(): pl.pallas_call(hand_over, out_shape=tuple((jax.ShapeDtypeStruct(x.shape,...  1.88 us

profile of v5, /device:TPU:0, one launch (start us, length us, event | category | flops | bytes accessed | tf_op | source)
XLA Modules:
  0.0 57.1 jit_solution(11639339452370950632)
XLA Ops:
  0.6 54.6 %graph_layer.1 = (bf16[512,256]{1,0:T(8,128)(2,1)}, bf16[512,256]{1,0:T(8,128)(2,1)}, f32[256,256]{1,0:T(8,128)}) custom-call(bf16[4,128,256]{2,1,0:T(8,128)(2,1)} %bitcast.3, bf16[256,256]{1,0:T(8,128)(2,1)} %weight_ref.1, bf16[1,5,4,128,128]{4,3,2,1,0:T(8,128)(2,1)} %tiles_ref.1, s32[1,4,5]{2,1,0:T(4,128)} %bitcast.4, s32[1,4,5]{2,1,0:T(4,128)} %bitcast.5, ...), custom_call_target="tpu_custom_call" | custom-call | tf_op jit(solution)/shard_map/graph_layer/pallas_call | solution.py:453
  55.3 1.9 %hand_over.1 = (bf16[512,256]{1,0:T(8,128)(2,1)}, bf16[512,256]{1,0:T(8,128)(2,1)}, f32[256,256]{1,0:T(8,128)}) custom-call(bf16[512,256]{1,0:T(8,128)(2,1)} %get-tuple-element.6.a, bf16[512,256]{1,0:T(8,128)(2,1)} %get-tuple-element.7.b, f32[256,256]{1,0:T(8,128)} %get-tuple-element.8.c), custom_call_target="tpu_custom_call" | custom-call | tf_op jit(solution)/shard_map/hand_over/pallas_call | solution.py:471

commit v6 on v5

--- a/solution.py
+++ b/solution.py
@@ -29,7 +29,7 @@
     part_send, part_recv, agg, pre, pre_grad, agg_grad,
     reply_send, back0, back1,
     g_own, g_send, g_recv,
-    wg_local, wg_rows, wg_chunk, wg_dom, wg_mine, act, grad,
+    wg_local, wg_send, wg_rows, wg_chunk, wg_pieces, wg_dom, wg_mine, wg_all, act, grad,
     load_sem, feat_ss, feat_rs, ids_ss, ids_rs, part_ss, part_rs, reply_ss, reply_rs,
     g_ss, g_rs, w1_ss, w1_rs, w2_ss, w2_rs, w3_ss, w3_rs, w4_ss, w4_rs, out_sem,
 ):
@@ -220,6 +220,25 @@
             reply_send.at[h, j], backs[h].at[rows], reply_ss.at[h, j], reply_rs.at[h, j], (d, row_at(-j))
         )
 
+    chunk = wg_rows.shape[1]
+
+    def w1_copy(j):
+        return remote(wg_send.at[row_at(j)], wg_rows.at[j], w1_ss.at[j], w1_rs.at[j], (d, row_at(j)))
+
+    def wg_first():
+        for h in range(halves):
+            wg_local[h * LANES:(h + 1) * LANES, :] = lax.dot_general(
+                agg[h], pre_grad[...], (((0,), (0,)), ((), ())), preferred_element_type=f32
+            )
+
+        @pl.loop(0, row_count)
+        def _(q):
+            wg_send[q] = wg_local[pl.ds(pl.multiple_of(q * chunk, chunk), chunk), :].astype(bf16)
+
+        @pl.loop(1, row_count)
+        def _(j):
+            w1_copy(j).start()
+
     for h in range(halves):
         product = dot(pre_grad[...], weight_t[:, h * LANES:(h + 1) * LANES])
         agg_grad[...] = product.astype(bf16)
@@ -238,50 +257,35 @@
 
         reply(0)
         backs[h][pl.ds(pl.multiple_of(r * cap, cap), cap)] = reply_send[h, 0]
-
-
-    for h in range(halves):
-        wg_local[h * LANES:(h + 1) * LANES, :] = lax.dot_general(
-            agg[h], pre_grad[...], (((0,), (0,)), ((), ())), preferred_element_type=f32
+        if h == 0:
+            wg_first()
+
+
+    pieces, high, wide = wg_pieces.shape
+    scatter = pieces > 1
+
+    def corner(i):
+        return slice(i // (wg_local.shape[1] // wide) * high, (i // (wg_local.shape[1] // wide) + 1) * high), slice(
+            i % (wg_local.shape[1] // wide) * wide, (i % (wg_local.shape[1] // wide) + 1) * wide
         )
-    chunk = wg_local.shape[0] // row_count
-
-    def w1_copy(j):
-        rows = pl.ds(pl.multiple_of(row_at(j) * chunk, chunk), chunk)
-        return remote(wg_local.at[rows], wg_rows.at[j], w1_ss.at[j], w1_rs.at[j], (d, row_at(j)))
-
-    @pl.loop(1, row_count)
-    def _(j):
-        w1_copy(j).start()
-
-    piece = chunk // dom_count
-    scatter = piece * dom_count == chunk and piece % 8 == 0
-    part = pl.ds(pl.multiple_of(d * piece, piece), piece)
 
     def w2_copy(j):
-        if scatter:
-            rows = pl.ds(pl.multiple_of(dom_at(j) * piece, piece), piece)
-            return remote(wg_chunk.at[rows], wg_dom.at[j], w2_ss.at[j], w2_rs.at[j], (dom_at(j), r))
-        return remote(wg_chunk, wg_dom.at[d], w2_ss.at[j], w2_rs.at[j], (dom_at(j), r))
+        src = wg_pieces.at[dom_at(j) if scatter else 0]
+        return remote(src, wg_dom.at[j], w2_ss.at[j], w2_rs.at[j], (dom_at(j), r))
 
     def w3_copy(j):
-        return remote(wg_mine.at[part], wg_mine.at[part], w3_ss.at[j], w3_rs.at[j], (dom_at(j), r))
+        return remote(wg_mine.at[d], wg_mine.at[d], w3_ss.at[j], w3_rs.at[j], (dom_at(j), r))
 
     def w4_copy(i, j):
-        span = piece if scatter else chunk
-        start = dom_at(-i) * piece if scatter else 0
-        src = wg_mine.at[pl.ds(pl.multiple_of(start, span), span)]
-        dst = wg_out.at[pl.ds(pl.multiple_of(r * chunk + start, span), span)]
-        return remote(src, dst, w4_ss.at[i, j], w4_rs.at[i, j], (d, row_at(j)))
+        at = dom_at(-i) if scatter else 0
+        return remote(wg_mine.at[at], wg_all.at[r, at], w4_ss.at[i, j], w4_rs.at[i, j], (d, row_at(j)))
 
     def w4_start(i):
         @pl.loop(1, row_count)
         def _(j):
             w4_copy(i, j).start()
 
-    wg_copy = pltpu.make_async_copy(
-        wg_mine, wg_out.at[pl.ds(pl.multiple_of(r * chunk, chunk), chunk)], out_sem.at[1 + halves]
-    )
+    wg_copy = pltpu.make_async_copy(wg_local, wg_out, out_sem.at[1 + halves])
 
     def wg_second():
         wg_chunk[...] = wg_local[pl.ds(pl.multiple_of(r * chunk, chunk), chunk), :]
@@ -289,7 +293,10 @@
         @pl.loop(1, row_count)
         def _(j):
             w1_copy(j).wait_recv()
-            wg_chunk[...] += wg_rows[j]
+            wg_chunk[...] += wg_rows[j].astype(f32)
+
+        for i in range(pieces):
+            wg_pieces[i] = wg_chunk[corner(i)].astype(bf16)
 
         @pl.loop(1, dom_count)
         def _(j):
@@ -328,11 +335,11 @@
             wg_second()
 
     if scatter:
-        total_own = wg_chunk[part, :]
+        total_own = wg_pieces[d].astype(f32)
         for j in range(1, dom_count):
             w2_copy(j).wait_recv()
-            total_own = total_own + wg_dom[j]
-        wg_mine[part, :] = total_own
+            total_own = total_own + wg_dom[j].astype(f32)
+        wg_mine[d] = total_own.astype(bf16)
 
         @pl.loop(1, dom_count)
         def _(j):
@@ -349,19 +356,16 @@
         def _(j):
             w3_copy(j).wait_send()
     else:
-        wg_dom[d] = wg_chunk[...]
+        wg_dom[0] = wg_pieces[0]
 
         @pl.loop(1, dom_count)
         def _(j):
             w2_copy(j).wait_recv()
 
-        wg_mine[...] = lax.fori_loop(
-            0, dom_count, lambda i, value: value + wg_dom[i], jnp.zeros(wg_chunk.shape, f32)
-        )
-
+        wg_mine[0] = lax.fori_loop(
+            0, dom_count, lambda i, value: value + wg_dom[dom_at(-i)].astype(f32), jnp.zeros(wg_chunk.shape, f32)
+        ).astype(bf16)
         w4_start(0)
-
-    wg_copy.start()
 
     def grad_copy(h):
         return pltpu.make_async_copy(grad.at[h], grad_out.at[:, pl.ds(h * LANES, LANES)], out_sem.at[1 + h])
@@ -380,6 +384,17 @@
         @pl.loop(1, row_count)
         def _(j):
             w4_copy(i, j).wait()
+
+    wg_all[r] = wg_mine[...]
+
+    @pl.loop(0, row_count)
+    def _(q):
+        for i in range(pieces):
+            rows, cols = corner(i)
+            here = pl.ds(pl.multiple_of(q * chunk + rows.start, high), high)
+            wg_local[here, cols] = wg_all[q, i].astype(f32)
+
+    wg_copy.start()
 
     act_copy.wait()
     wg_copy.wait()
@@ -426,8 +441,8 @@
     slots = slot_block.shape[1]
     cap = slots // row_count
     chunk = channels // row_count
-    piece = chunk // dom_count
-    scatter = piece * dom_count == chunk and piece % 8 == 0
+    scatter = chunk % 16 == 0 and chunk // 16 * halves == dom_count
+    pieces, piece = (dom_count, (16, LANES)) if scatter else (1, (chunk, channels))
     smem = pl.BlockSpec(memory_space=pltpu.SMEM)
     anywhere = pl.BlockSpec(memory_space=pl.ANY)
     V = pltpu.VMEM
@@ -441,8 +456,9 @@
         V((halves, nodes, LANES), bf16), V((nodes, channels), f32), V((nodes, channels), bf16), V((nodes, LANES), bf16),
         V((halves, row_count, cap, B, LANES), bf16), V((slots, B, LANES), bf16), V((slots, B, LANES), bf16),
         V((halves, nodes, LANES), f32), V((halves, 5, nodes, LANES), bf16), V((halves, 5, nodes, LANES), bf16),
-        V((channels, channels), f32), V((row_count, chunk, channels), f32), V((chunk, channels), f32),
-        V((dom_count, piece if scatter else chunk, channels), f32), V((chunk, channels), f32),
+        V((channels, channels), f32), V((row_count, chunk, channels), bf16), V((row_count, chunk, channels), bf16),
+        V((chunk, channels), f32), V((pieces, *piece), bf16), V((dom_count, *piece), bf16), V((pieces, *piece), bf16),
+        V((row_count, pieces, *piece), bf16),
         V((nodes, channels), bf16), V((halves, nodes, LANES), bf16),
         dma((3 + halves,)), dma((halves, 5)), dma((halves, 5)), dma((row_count,)), dma((row_count,)),
         dma((halves, row_count)), dma((halves, row_count)), dma((halves, row_count)), dma((halves, row_count)),

time: 57.3 us -> 55.9 us (0.976)
  Pallas kernels: 56.5 us -> 55.1 us
    pallas_call x1, Pallas kernels: 54.6 us -> 53.2 us  [per_device(): pl.pallas_call(functools.partial(kernel, dom_count, row_count), out_shape...]
where the time goes in v6:
time: 55.9 us; the launch traced here: 55.7 us
  Pallas kernels  55.1 us (99%)
  between operations  0.64 us (1%)
    pallas_call x1, Pallas kernels, per_device(): pl.pallas_call(functools.partial(kernel, dom_count, row_count), out_shape...  53.2 us
    pallas_call x1, Pallas kernels, per_device(): pl.pallas_call(hand_over, out_shape=tuple((jax.ShapeDtypeStruct(x.shape,...  1.88 us

profile of v6, /device:TPU:0, one launch (start us, length us, event | category | flops | bytes accessed | tf_op | source)
XLA Modules:
  0.0 55.7 jit_solution(11905505584033911081)
XLA Ops:
  0.6 53.2 %graph_layer.1 = (bf16[512,256]{1,0:T(8,128)(2,1)}, bf16[512,256]{1,0:T(8,128)(2,1)}, f32[256,256]{1,0:T(8,128)}) custom-call(bf16[4,128,256]{2,1,0:T(8,128)(2,1)} %bitcast.3, bf16[256,256]{1,0:T(8,128)(2,1)} %weight_ref.1, bf16[1,5,4,128,128]{4,3,2,1,0:T(8,128)(2,1)} %tiles_ref.1, s32[1,4,5]{2,1,0:T(4,128)} %bitcast.4, s32[1,4,5]{2,1,0:T(4,128)} %bitcast.5, ...), custom_call_target="tpu_custom_call" | custom-call | tf_op jit(solution)/shard_map/graph_layer/pallas_call | solution.py:469
  53.9 1.9 %hand_over.1 = (bf16[512,256]{1,0:T(8,128)(2,1)}, bf16[512,256]{1,0:T(8,128)(2,1)}, f32[256,256]{1,0:T(8,128)}) custom-call(bf16[512,256]{1,0:T(8,128)(2,1)} %get-tuple-element.6.a, bf16[512,256]{1,0:T(8,128)(2,1)} %get-tuple-element.7.b, f32[256,256]{1,0:T(8,128)} %get-tuple-element.8.c), custom_call_target="tpu_custom_call" | custom-call | tf_op jit(solution)/shard_map/hand_over/pallas_call | solution.py:487

commit v7 on v6

--- a/solution.py
+++ b/solution.py
@@ -22,14 +22,14 @@
 def kernel(
     dom_count, row_count,
     feat_ref, weight_ref, tiles_ref, source_ref, slot_ref, block_ref, count_ref, cot_ref,
-    act_out, grad_out, wg_out,
+    act_out, own_out, grad_out, wg_out,
     tiles, tiles_t, weight, weight_t, cot, prod, acc,
     own0, near0, far0, mate0, passed0, own1, near1, far1, mate1, passed1,
     ids_send, ids_recv,
     part_send, part_recv, agg, pre, pre_grad, agg_grad,
     reply_send, back0, back1,
     g_own, g_send, g_recv,
-    wg_local, wg_send, wg_rows, wg_chunk, wg_pieces, wg_dom, wg_mine, wg_all, act, grad,
+    wg_local, wg_send, wg_rows, wg_chunk, wg_pieces, wg_dom, wg_mine, act,
     load_sem, feat_ss, feat_rs, ids_ss, ids_rs, part_ss, part_rs, reply_ss, reply_rs,
     g_ss, g_rs, w1_ss, w1_rs, w2_ss, w2_rs, w3_ss, w3_rs, w4_ss, w4_rs, out_sem,
 ):
@@ -265,9 +265,7 @@
     scatter = pieces > 1
 
     def corner(i):
-        return slice(i // (wg_local.shape[1] // wide) * high, (i // (wg_local.shape[1] // wide) + 1) * high), slice(
-            i % (wg_local.shape[1] // wide) * wide, (i % (wg_local.shape[1] // wide) + 1) * wide
-        )
+        return corner_of(i, wg_local.shape[1], high, wide)
 
     def w2_copy(j):
         src = wg_pieces.at[dom_at(j) if scatter else 0]
@@ -278,14 +276,14 @@
 
     def w4_copy(i, j):
         at = dom_at(-i) if scatter else 0
-        return remote(wg_mine.at[at], wg_all.at[r, at], w4_ss.at[i, j], w4_rs.at[i, j], (d, row_at(j)))
+        return remote(wg_mine.at[at], wg_out.at[r, at], w4_ss.at[i, j], w4_rs.at[i, j], (d, row_at(j)))
 
     def w4_start(i):
         @pl.loop(1, row_count)
         def _(j):
             w4_copy(i, j).start()
 
-    wg_copy = pltpu.make_async_copy(wg_local, wg_out, out_sem.at[1 + halves])
+    wg_copy = pltpu.make_async_copy(wg_mine, wg_out.at[r], out_sem.at[1 + halves])
 
     def wg_second():
         wg_chunk[...] = wg_local[pl.ds(pl.multiple_of(r * chunk, chunk), chunk), :]
@@ -304,7 +302,11 @@
 
     def g_copy(h, role):
         device = {NEAR: up_dev, FAR: down_dev, MATE: mate_dev, PASSED: mate_dev}[role]
-        return remote(g_send.at[h, role], g_recv.at[h, role], g_ss.at[h, role], g_rs.at[h, role], device)
+        target = g_recv.at[h] if role == PASSED else grad_out.at[h, role - 1]
+        return remote(g_send.at[h, role], target, g_ss.at[h, role], g_rs.at[h, role], device)
+
+    def own_copy(h):
+        return pltpu.make_async_copy(g_own.at[h], own_out.at[h], out_sem.at[1 + h])
 
     for h in range(halves):
         @pl.loop(1, row_count)
@@ -326,11 +328,12 @@
             source_terms(role, g_send.at[h, role])
             g_copy(h, role).start()
         g_copy(h, PASSED).wait_recv()
-        source_terms(NEAR, g_send.at[h, NEAR], g_recv.at[h, PASSED])
+        source_terms(NEAR, g_send.at[h, NEAR], g_recv.at[h])
         g_copy(h, NEAR).start()
         source_terms(MATE, g_send.at[h, MATE])
         g_copy(h, MATE).start()
         source_terms(OWN, g_own.at[h])
+        own_copy(h).start()
         if h == 0:
             wg_second()
 
@@ -367,17 +370,11 @@
         ).astype(bf16)
         w4_start(0)
 
-    def grad_copy(h):
-        return pltpu.make_async_copy(grad.at[h], grad_out.at[:, pl.ds(h * LANES, LANES)], out_sem.at[1 + h])
+    wg_copy.start()
 
     for h in range(halves):
         for role in (MATE, NEAR, FAR):
             g_copy(h, role).wait_recv()
-        value = g_own[h]
-        for role in (MATE, NEAR, FAR):
-            value = value + g_recv[h, role].astype(f32)
-        grad[h] = value.astype(bf16)
-        grad_copy(h).start()
 
     @pl.loop(0, dom_count if scatter else 1)
     def _(i):
@@ -385,16 +382,6 @@
         def _(j):
             w4_copy(i, j).wait()
 
-    wg_all[r] = wg_mine[...]
-
-    @pl.loop(0, row_count)
-    def _(q):
-        for i in range(pieces):
-            rows, cols = corner(i)
-            here = pl.ds(pl.multiple_of(q * chunk + rows.start, high), high)
-            wg_local[here, cols] = wg_all[q, i].astype(f32)
-
-    wg_copy.start()
 
     act_copy.wait()
     wg_copy.wait()
@@ -402,7 +389,7 @@
         for role in (NEAR, FAR, MATE, PASSED):
             feat_copy(h, role).wait_send()
             g_copy(h, role).wait_send()
-        grad_copy(h).wait()
+        own_copy(h).wait()
 
         @pl.loop(1, row_count)
         def _(j):
@@ -418,15 +405,45 @@
         w2_copy(j).wait_send()
 
 
-def hand_over(a, b, c, to_a, to_b, to_c, in_a, in_b, in_c, sem):
-    triples = ((a, in_a, to_a), (b, in_b, to_b), (c, in_c, to_c))
-    reads = [pltpu.make_async_copy(x, y, sem.at[0, i]) for i, (x, y, _) in enumerate(triples)]
-    writes = [pltpu.make_async_copy(y, z, sem.at[1, i]) for i, (_, y, z) in enumerate(triples)]
+def corner_of(i, channels, high, wide):
+    across = channels // wide
+    row, column = i // across * high, i % across * wide
+    return slice(row, row + high), slice(column, column + wide)
+
+
+def hand_over(act, own, grad, wg, to_act, to_grad, to_wg, in_act, in_own, in_grad, in_wg, sums, full, sem, out_sem):
+    halves = own.shape[0]
+    row_count, pieces, high, wide = wg.shape
+    channels = full.shape[0]
+    reads = []
+    for h in range(halves):
+        reads.append(pltpu.make_async_copy(own.at[h], in_own.at[h], sem.at[2 * h]))
+        reads.append(pltpu.make_async_copy(grad.at[h], in_grad.at[h], sem.at[2 * h + 1]))
+    reads.append(pltpu.make_async_copy(act, in_act, sem.at[2 * halves]))
+    reads.append(pltpu.make_async_copy(wg, in_wg, sem.at[2 * halves + 1]))
     for copy in reads:
         copy.start()
-    for read, write in zip(reads, writes):
-        read.wait()
-        write.start()
+    writes = []
+    for h in range(halves):
+        reads[2 * h].wait()
+        reads[2 * h + 1].wait()
+        value = in_own[h]
+        for i in (2, 0, 1):
+            value = value + in_grad[h, i].astype(f32)
+        sums[h] = value.astype(bf16)
+        writes.append(pltpu.make_async_copy(sums.at[h], to_grad.at[:, pl.ds(h * LANES, LANES)], out_sem.at[h]))
+        writes[-1].start()
+    reads[-2].wait()
+    writes.append(pltpu.make_async_copy(in_act, to_act, out_sem.at[halves]))
+    writes[-1].start()
+    reads[-1].wait()
+    chunk = channels // row_count
+    for q in range(row_count):
+        for i in range(pieces):
+            rows, cols = corner_of(i, channels, high, wide)
+            full[q * chunk + rows.start:q * chunk + rows.stop, cols] = in_wg[q, i].astype(f32)
+    writes.append(pltpu.make_async_copy(full, to_wg, out_sem.at[halves + 1]))
+    writes[-1].start()
     for copy in writes:
         copy.wait()
 
@@ -455,11 +472,10 @@
         V((halves, row_count, cap * B, LANES), bf16), V((halves, row_count, cap * B, LANES), bf16),
         V((halves, nodes, LANES), bf16), V((nodes, channels), f32), V((nodes, channels), bf16), V((nodes, LANES), bf16),
         V((halves, row_count, cap, B, LANES), bf16), V((slots, B, LANES), bf16), V((slots, B, LANES), bf16),
-        V((halves, nodes, LANES), f32), V((halves, 5, nodes, LANES), bf16), V((halves, 5, nodes, LANES), bf16),
+        V((halves, nodes, LANES), f32), V((halves, 5, nodes, LANES), bf16), V((halves, nodes, LANES), bf16),
         V((channels, channels), f32), V((row_count, chunk, channels), bf16), V((row_count, chunk, channels), bf16),
         V((chunk, channels), f32), V((pieces, *piece), bf16), V((dom_count, *piece), bf16), V((pieces, *piece), bf16),
-        V((row_count, pieces, *piece), bf16),
-        V((nodes, channels), bf16), V((halves, nodes, LANES), bf16),
+        V((nodes, channels), bf16),
         dma((3 + halves,)), dma((halves, 5)), dma((halves, 5)), dma((row_count,)), dma((row_count,)),
         dma((halves, row_count)), dma((halves, row_count)), dma((halves, row_count)), dma((halves, row_count)),
         dma((halves, 5)), dma((halves, 5)),
@@ -470,11 +486,12 @@
         functools.partial(kernel, dom_count, row_count),
         out_shape=(
             jax.ShapeDtypeStruct((nodes, channels), bf16),
-            jax.ShapeDtypeStruct((nodes, channels), bf16),
-            jax.ShapeDtypeStruct((channels, channels), f32),
+            jax.ShapeDtypeStruct((halves, nodes, LANES), f32),
+            jax.ShapeDtypeStruct((halves, 3, nodes, LANES), bf16),
+            jax.ShapeDtypeStruct((row_count, pieces, *piece), bf16),
         ),
         in_specs=[anywhere, anywhere, anywhere, smem, smem, smem, smem, anywhere],
-        out_specs=(anywhere, anywhere, anywhere),
+        out_specs=(anywhere,) * 4,
         scratch_shapes=scratch,
         compiler_params=pltpu.CompilerParams(
             collective_id=0, has_side_effects=True, vmem_limit_bytes=56 * 1024 * 1024
@@ -486,10 +503,17 @@
     )
     return pl.pallas_call(
         hand_over,
-        out_shape=tuple(jax.ShapeDtypeStruct(x.shape, x.dtype) for x in results),
-        in_specs=[anywhere] * 3,
+        out_shape=(
+            jax.ShapeDtypeStruct((nodes, channels), bf16),
+            jax.ShapeDtypeStruct((nodes, channels), bf16),
+            jax.ShapeDtypeStruct((channels, channels), f32),
+        ),
+        in_specs=[anywhere] * 4,
         out_specs=(anywhere,) * 3,
-        scratch_shapes=[*[V(x.shape, x.dtype) for x in results], dma((2, 3))],
+        scratch_shapes=[
+            *[V(x.shape, x.dtype) for x in results],
+            V((halves, nodes, LANES), bf16), V((channels, channels), f32), dma((2 * halves + 2,)), dma((halves + 2,)),
+        ],
         compiler_params=pltpu.CompilerParams(vmem_limit_bytes=60 * 1024 * 1024),
         name="hand_over",
     )(*results)

time: 55.9 us -> 55.7 us (level)
  no operation moved by 1% of the time
where the time goes in v7:
time: 55.7 us; the launch traced here: 55.6 us
  Pallas kernels  54.9 us (99%)
  between operations  0.64 us (1%)
    pallas_call x1, Pallas kernels, per_device(): pl.pallas_call(functools.partial(kernel, dom_count, row_count), out_shape...  52.7 us
    pallas_call x1, Pallas kernels, per_device(): pl.pallas_call(hand_over, out_shape=(jax.ShapeDtypeStruct((nodes, channel...  2.25 us

profile of v7, /device:TPU:0, one launch (start us, length us, event | category | flops | bytes accessed | tf_op | source)
XLA Modules:
  0.0 55.6 jit_solution(4695271777746714565)
XLA Ops:
  0.6 52.7 %graph_layer.1 = (bf16[512,256]{1,0:T(8,128)(2,1)}, f32[2,512,128]{2,1,0:T(8,128)}, bf16[2,3,512,128]{3,2,1,0:T(8,128)(2,1)}, bf16[4,8,16,128]{3,2,1,0:T(8,128)(2,1)}) custom-call(bf16[4,128,256]{2,1,0:T(8,128)(2,1)} %bitcast.3, bf16[256,256]{1,0:T(8,128)(2,1)} %weight_ref.1, bf16[1,5,4,128,128]{4,3,2,1,0:T(8,128)(2,1)} %tiles_ref.1, s32[1,4,5]{2,1,0:T(4,128)} %bitcast.4, ...), custom_call_target="tpu_custom_call" | custom-call | tf_op jit(solution)/shard_map/graph_layer/pallas_call | solution.py:485
  53.3 2.3 %hand_over.1 = (bf16[512,256]{1,0:T(8,128)(2,1)}, bf16[512,256]{1,0:T(8,128)(2,1)}, f32[256,256]{1,0:T(8,128)}) custom-call(bf16[512,256]{1,0:T(8,128)(2,1)} %get-tuple-element.7.act, f32[2,512,128]{2,1,0:T(8,128)} %get-tuple-element.8.own, bf16[2,3,512,128]{3,2,1,0:T(8,128)(2,1)} %get-tuple-element.9.grad, bf16[4,8,16,128]{3,2,1,0:T(8,128)(2,1)} %get-tuple-element.10.wg), custom_call_target="tpu_custom_call" | custom-call | tf_op jit(solution)/shard_map/hand_over/pallas_call | solution.py:504

commit v8 on v7

--- a/solution.py
+++ b/solution.py
@@ -84,7 +84,7 @@
         copy.start()
     pl.semaphore_wait(barrier, dom_count + row_count - 2)
 
-    def feat_copy(h, role):
+    def feat_copy(h, role, b=None):
         own = columns(h)
         if role == PASSED:
             src, device = feats[h][NEAR], mate_dev
@@ -94,10 +94,20 @@
             src, device = own, up_dev
         else:
             src, device = own, down_dev
-        return remote(src, feats[h][role], feat_ss.at[h, role], feat_rs.at[h, role], device)
-
-    for h in range(halves):
-        for role in (NEAR, FAR, MATE):
+        if b is None:
+            return remote(src, feats[h][role], feat_ss.at[h, role, 0], feat_rs.at[h, role, 0], device)
+        if role == NEAR:
+            src = feat_ref.at[b, :, pl.ds(h * LANES, LANES)]
+        else:
+            src = src.at[b]
+        return remote(src, feats[h][role].at[b], feat_ss.at[h, role, b], feat_rs.at[h, role, b], device)
+
+    for h in range(halves):
+        @pl.loop(0, nblk)
+        def _(b):
+            feat_copy(h, NEAR, b).start()
+
+        for role in (FAR, MATE):
             feat_copy(h, role).start()
 
     @pl.loop(0, row_count)
@@ -155,14 +165,22 @@
 
     for h in range(halves):
         add_role(h, OWN, True)
-        feat_copy(h, NEAR).wait_recv()
-        feat_copy(h, PASSED).start()
+
+        @pl.loop(0, nblk)
+        def _(b):
+            feat_copy(h, NEAR, b).wait_recv()
+            feat_copy(h, PASSED, b).start()
+
         feat_copy(h, MATE).wait_recv()
         add_role(h, MATE, False)
         add_role(h, NEAR, False)
         feat_copy(h, FAR).wait_recv()
         add_role(h, FAR, False)
-        feat_copy(h, PASSED).wait_recv()
+
+        @pl.loop(0, nblk)
+        def _(b):
+            feat_copy(h, PASSED, b).wait_recv()
+
         products(tiles, feats[h][PASSED], source_ref, PASSED)
 
         def finish(q):
@@ -300,10 +318,13 @@
         def _(j):
             w2_copy(j).start()
 
-    def g_copy(h, role):
+    def g_copy(h, role, b=None):
         device = {NEAR: up_dev, FAR: down_dev, MATE: mate_dev, PASSED: mate_dev}[role]
         target = g_recv.at[h] if role == PASSED else grad_out.at[h, role - 1]
-        return remote(g_send.at[h, role], target, g_ss.at[h, role], g_rs.at[h, role], device)
+        if b is None:
+            return remote(g_send.at[h, role], target, g_ss.at[h, role, 0], g_rs.at[h, role, 0], device)
+        rows = pl.ds(pl.multiple_of(b * B, B), B)
+        return remote(g_send.at[h, role, rows], target.at[rows], g_ss.at[h, role, b], g_rs.at[h, role, b], device)
 
     def own_copy(h):
         return pltpu.make_async_copy(g_own.at[h], own_out.at[h], out_sem.at[1 + h])
@@ -313,23 +334,24 @@
         def _(j):
             reply_copy(h, j).wait_recv()
 
-        def source_terms(role, target, extra=None):
+        def source_terms(role, target):
             products(tiles_t, backs[h], slot_ref, role)
 
             @pl.loop(0, nblk)
             def _(b):
                 rows = pl.ds(pl.multiple_of(b * B, B), B)
                 value = mixed(source_ref, role, b)
-                if extra is not None:
-                    value = value + extra[rows, :].astype(f32)
+                if role == NEAR:
+                    g_copy(h, PASSED, b).wait_recv()
+                    value = value + g_recv[h, rows, :].astype(f32)
                 target[rows, :] = value.astype(target.dtype)
-
-        for role in (PASSED, FAR):
-            source_terms(role, g_send.at[h, role])
-            g_copy(h, role).start()
-        g_copy(h, PASSED).wait_recv()
-        source_terms(NEAR, g_send.at[h, NEAR], g_recv.at[h])
-        g_copy(h, NEAR).start()
+                if role in (PASSED, NEAR):
+                    g_copy(h, role, b).start()
+
+        source_terms(PASSED, g_send.at[h, PASSED])
+        source_terms(FAR, g_send.at[h, FAR])
+        g_copy(h, FAR).start()
+        source_terms(NEAR, g_send.at[h, NEAR])
         source_terms(MATE, g_send.at[h, MATE])
         g_copy(h, MATE).start()
         source_terms(OWN, g_own.at[h])
@@ -373,8 +395,13 @@
     wg_copy.start()
 
     for h in range(halves):
-        for role in (MATE, NEAR, FAR):
+        for role in (MATE, FAR):
             g_copy(h, role).wait_recv()
+
+        @pl.loop(0, nblk)
+        def _(b):
+            g_copy(h, NEAR, b).wait_recv()
+
 
     @pl.loop(0, dom_count if scatter else 1)
     def _(i):
@@ -386,9 +413,16 @@
     act_copy.wait()
     wg_copy.wait()
     for h in range(halves):
-        for role in (NEAR, FAR, MATE, PASSED):
+        for role in (FAR, MATE):
             feat_copy(h, role).wait_send()
             g_copy(h, role).wait_send()
+
+        @pl.loop(0, nblk)
+        def _(b):
+            for role in (NEAR, PASSED):
+                feat_copy(h, role, b).wait_send()
+                g_copy(h, role, b).wait_send()
+
         own_copy(h).wait()
 
         @pl.loop(1, row_count)
@@ -476,9 +510,9 @@
         V((channels, channels), f32), V((row_count, chunk, channels), bf16), V((row_count, chunk, channels), bf16),
         V((chunk, channels), f32), V((pieces, *piece), bf16), V((dom_count, *piece), bf16), V((pieces, *piece), bf16),
         V((nodes, channels), bf16),
-        dma((3 + halves,)), dma((halves, 5)), dma((halves, 5)), dma((row_count,)), dma((row_count,)),
+        dma((3 + halves,)), dma((halves, 5, nblk)), dma((halves, 5, nblk)), dma((row_count,)), dma((row_count,)),
         dma((halves, row_count)), dma((halves, row_count)), dma((halves, row_count)), dma((halves, row_count)),
-        dma((halves, 5)), dma((halves, 5)),
+        dma((halves, 5, nblk)), dma((halves, 5, nblk)),
         dma((row_count,)), dma((row_count,)), dma((dom_count,)), dma((dom_count,)),
         dma((dom_count,)), dma((dom_count,)), dma((dom_count, row_count)), dma((dom_count, row_count)), dma((2 + halves,)),
     ]

time: 55.7 us -> 57 us (1.023)
  Pallas kernels: 54.9 us -> 56.1 us
    pallas_call x1, Pallas kernels: 52.7 us -> 53.9 us  [per_device(): pl.pallas_call(functools.partial(kernel, dom_count, row_count), out_shape...]
where the time goes in v8:
time: 57 us; the launch traced here: 56.8 us
  Pallas kernels  56.1 us (98%)
  between operations  0.64 us (1%)
    pallas_call x1, Pallas kernels, per_device(): pl.pallas_call(functools.partial(kernel, dom_count, row_count), out_shape...  53.9 us
    pallas_call x1, Pallas kernels, per_device(): pl.pallas_call(hand_over, out_shape=(jax.ShapeDtypeStruct((nodes, channel...  2.25 us

profile of v8, /device:TPU:0, one launch (start us, length us, event | category | flops | bytes accessed | tf_op | source)
XLA Modules:
  0.0 56.8 jit_solution(584166055098506305)
XLA Ops:
  0.6 53.9 %graph_layer.1 = (bf16[512,256]{1,0:T(8,128)(2,1)}, f32[2,512,128]{2,1,0:T(8,128)}, bf16[2,3,512,128]{3,2,1,0:T(8,128)(2,1)}, bf16[4,8,16,128]{3,2,1,0:T(8,128)(2,1)}) custom-call(bf16[4,128,256]{2,1,0:T(8,128)(2,1)} %bitcast.3, bf16[256,256]{1,0:T(8,128)(2,1)} %weight_ref.1, bf16[1,5,4,128,128]{4,3,2,1,0:T(8,128)(2,1)} %tiles_ref.1, s32[1,4,5]{2,1,0:T(4,128)} %bitcast.4, ...), custom_call_target="tpu_custom_call" | custom-call | tf_op jit(solution)/shard_map/graph_layer/pallas_call | solution.py:519
  54.5 2.3 %hand_over.1 = (bf16[512,256]{1,0:T(8,128)(2,1)}, bf16[512,256]{1,0:T(8,128)(2,1)}, f32[256,256]{1,0:T(8,128)}) custom-call(bf16[512,256]{1,0:T(8,128)(2,1)} %get-tuple-element.7.act, f32[2,512,128]{2,1,0:T(8,128)} %get-tuple-element.8.own, bf16[2,3,512,128]{3,2,1,0:T(8,128)(2,1)} %get-tuple-element.9.grad, bf16[4,8,16,128]{3,2,1,0:T(8,128)(2,1)} %get-tuple-element.10.wg), custom_call_target="tpu_custom_call" | custom-call | tf_op jit(solution)/shard_map/hand_over/pallas_call | solution.py:538

commit v9 on v7

--- a/solution.py
+++ b/solution.py
@@ -80,12 +80,14 @@
     ]
     for h in range(halves):
         loads.append(pltpu.make_async_copy(columns(h), feats[h][OWN], load_sem.at[3 + h]))
-    for copy in loads:
+    for copy in loads[3:] + loads[:3]:
         copy.start()
+    for copy in loads[3:]:
+        copy.wait()
     pl.semaphore_wait(barrier, dom_count + row_count - 2)
 
     def feat_copy(h, role):
-        own = columns(h)
+        own = feats[h][OWN]
         if role == PASSED:
             src, device = feats[h][NEAR], mate_dev
         elif role == MATE:
@@ -114,7 +116,7 @@
     def _(j):
         ids_copy(j).start()
 
-    for copy in loads:
+    for copy in loads[:3]:
         copy.wait()
 
     def live(role, t):

time: 55.7 us -> 55.5 us (level)
  no operation moved by 1% of the time
where the time goes in v9:
time: 55.5 us; the launch traced here: 55.3 us
  Pallas kernels  54.7 us (99%)
  between operations  0.64 us (1%)
    pallas_call x1, Pallas kernels, per_device(): pl.pallas_call(functools.partial(kernel, dom_count, row_count), out_shape...  52.5 us
    pallas_call x1, Pallas kernels, per_device(): pl.pallas_call(hand_over, out_shape=(jax.ShapeDtypeStruct((nodes, channel...  2.25 us

profile of v9, /device:TPU:0, one launch (start us, length us, event | category | flops | bytes accessed | tf_op | source)
XLA Modules:
  0.0 55.3 jit_solution(12997544772975774752)
XLA Ops:
  0.6 52.5 %graph_layer.1 = (bf16[512,256]{1,0:T(8,128)(2,1)}, f32[2,512,128]{2,1,0:T(8,128)}, bf16[2,3,512,128]{3,2,1,0:T(8,128)(2,1)}, bf16[4,8,16,128]{3,2,1,0:T(8,128)(2,1)}) custom-call(bf16[4,128,256]{2,1,0:T(8,128)(2,1)} %bitcast.3, bf16[256,256]{1,0:T(8,128)(2,1)} %weight_ref.1, bf16[1,5,4,128,128]{4,3,2,1,0:T(8,128)(2,1)} %tiles_ref.1, s32[1,4,5]{2,1,0:T(4,128)} %bitcast.4, ...), custom_call_target="tpu_custom_call" | custom-call | tf_op jit(solution)/shard_map/graph_layer/pallas_call | solution.py:487
  53.1 2.3 %hand_over.1 = (bf16[512,256]{1,0:T(8,128)(2,1)}, bf16[512,256]{1,0:T(8,128)(2,1)}, f32[256,256]{1,0:T(8,128)}) custom-call(bf16[512,256]{1,0:T(8,128)(2,1)} %get-tuple-element.7.act, f32[2,512,128]{2,1,0:T(8,128)} %get-tuple-element.8.own, bf16[2,3,512,128]{3,2,1,0:T(8,128)(2,1)} %get-tuple-element.9.grad, bf16[4,8,16,128]{3,2,1,0:T(8,128)(2,1)} %get-tuple-element.10.wg), custom_call_target="tpu_custom_call" | custom-call | tf_op jit(solution)/shard_map/hand_over/pallas_call | solution.py:506
